TPU v7x, 32 devices: a whole 2x2x4 slice. The times are simulated.
32 devices in a mesh: seg: 8 (over z, y), rep: 4 (over x, core).
Axes of the slice: x: 2, y: 2, z: 4, core: 2. Of those that a mesh axis runs over, the one named last changes fastest.
Arguments:
- tokens: bfloat16 [4, 2048, 1024], P('rep', 'seg'), may hold values from -6 to 6
- cotangent: bfloat16 [4, 2048, 1024], P('rep', 'seg'), may hold values from -6 to 6
- coefficients: bfloat16 [4, 8, 32], P('rep'), may hold values from 0 to 1, as said below
- w_gate: bfloat16 [32, 1024, 512], P(None, 'seg'), may hold values from -0.1875 to 0.1875
- w_up: bfloat16 [32, 1024, 512], P(None, 'seg'), may hold values from -0.1875 to 0.1875
- w_down: bfloat16 [32, 1024, 512], P(None, 'seg'), may hold values from -0.25 to 0.25
Outputs:
- input_grad: bfloat16 [4, 2048, 1024], P('rep', 'seg')
- grad_gate: bfloat16 [32, 1024, 512], P('rep', 'seg')
- grad_up: bfloat16 [32, 1024, 512], P('rep', 'seg')
- grad_down: bfloat16 [32, 1024, 512], P('rep', 'seg')
Inputs may be any that keep to these rules, and one draw needn't show every extreme that they name: Each segment's coefficients are positive and sum to 1 over the 32 experts, up to bfloat16 rounding.
All inputs are finite; a program needn't handle non-finite values.
Results may differ from a plain program's by a relative error of at most 0.0072.
Values may be sent and summed in bfloat16 or wider, within the bound.
A program may use at most 128 MiB of HBM per device.

v0:
```python
import jax
import jax.numpy as jnp
from jax import lax
from jax.sharding import PartitionSpec as P


def local(tokens, cotangent, coefficients, w_gate, w_up, w_down):
    mixing = coefficients[0]
    stacked = jnp.stack([w_gate, w_up, w_down])
    merged = jnp.einsum(
        "se,kedh->ksdh", mixing, stacked, preferred_element_type=jnp.float32
    ).astype(jnp.bfloat16)
    arrived = lax.all_to_all(merged, "seg", split_axis=1, concat_axis=2, tiled=True)
    merged_gate = arrived[0, 0]
    merged_up = arrived[1, 0]
    merged_down = arrived[2, 0]
    segment_x = tokens[0]
    segment_g = cotangent[0]
    contract = (((0,), (0,)), ((), ()))
    transposed = (((1,), (1,)), ((), ()))

    def fold_experts(pieces):
        return jnp.einsum("se,ksdh->kedh", mixing, pieces, preferred_element_type=jnp.float32)

    gate_proj = jnp.dot(segment_x, merged_gate, preferred_element_type=jnp.float32)
    up_proj = jnp.dot(segment_x, merged_up, preferred_element_type=jnp.float32)
    sigma = jax.nn.sigmoid(gate_proj)
    activated = gate_proj * sigma
    hidden = (activated * up_proj).astype(jnp.bfloat16)
    grad_down_seg = lax.dot_general(
        segment_g, hidden, contract, preferred_element_type=jnp.float32
    ).astype(jnp.bfloat16)
    down_folded = fold_experts(
        lax.all_to_all(grad_down_seg[None, None], "seg", split_axis=2, concat_axis=1, tiled=True)
    )
    down_summed = lax.psum_scatter(down_folded, "rep", scatter_dimension=1, tiled=True)
    d_hidden = jnp.dot(segment_g, merged_down, preferred_element_type=jnp.float32)
    d_gate = (d_hidden * up_proj * sigma * (1.0 + gate_proj * (1.0 - sigma))).astype(jnp.bfloat16)
    d_up = (d_hidden * activated).astype(jnp.bfloat16)
    input_grad = lax.dot_general(
        d_gate, merged_gate, transposed, preferred_element_type=jnp.float32
    )
    input_grad = input_grad + lax.dot_general(
        d_up, merged_up, transposed, preferred_element_type=jnp.float32
    )
    input_grad = input_grad.astype(jnp.bfloat16)
    grad_gate_seg = lax.dot_general(
        segment_x, d_gate, contract, preferred_element_type=jnp.float32
    ).astype(jnp.bfloat16)
    grad_up_seg = lax.dot_general(
        segment_x, d_up, contract, preferred_element_type=jnp.float32
    ).astype(jnp.bfloat16)
    pair = jnp.stack([grad_gate_seg, grad_up_seg])[:, None]
    pair_folded = fold_experts(lax.all_to_all(pair, "seg", split_axis=2, concat_axis=1, tiled=True))
    pair_summed = lax.psum_scatter(pair_folded, "rep", scatter_dimension=1, tiled=True)
    summed = jnp.concatenate([pair_summed, down_summed], axis=0)
    grads = summed.astype(jnp.bfloat16)
    return (input_grad[None], grads[0], grads[1], grads[2])


def solution(mesh):
    placed = (
        P("rep", "seg", None),
        P("rep", "seg", None),
        P("rep", None, None),
        P(None, "seg", None),
        P(None, "seg", None),
        P(None, "seg", None),
    )
    return jax.shard_map(
        local,
        mesh=mesh,
        in_specs=placed,
        out_specs=(
            P("rep", "seg", None),
            P("rep", "seg", None),
            P("rep", "seg", None),
            P("rep", "seg", None),
        ),
        check_vma=False,
    )
```

profile of v0, /device:TPU:21, one launch (start us, length us, event | category | flops | bytes accessed | tf_op | source)
XLA Modules:
  0.0 378.0 jit_solution(17529994948225392822)
XLA Ops:
  7.2 0.0 copy-start
  7.2 0.0 reduce-scatter.5.cloned.1.call-start
  7.2 0.0 copy-start.1
  7.2 0.0 copy-start.2
  7.2 4.7 %copy.70 = bf16[32,128,512]{2,0,1:T(8,128)(2,1)S(1)} copy(bf16[32,128,512]{2,1,0:T(8,128)(2,1)} %param.9) | data formatting | bytes 8388608 | tf_op args[3]
  11.9 0.0 copy-done.1
  11.9 0.1 copy-done.2
  12.0 10.3 %copy_bitcast_fusion = (bf16[1,32,128,512]{3,1,2,0:T(8,128)(2,1)S(1)}, bf16[1,32,128,512]{3,1,2,0:T(8,128)(2,1)S(1)}) fusion(bf16[32,128,512]{2,1,0:T(8,128)(2,1)S(1)} %copy-done.1, bf16[32,128,512]{2,1,0:T(8,128)(2,1)S(1)} %copy-done.2), kind=kLoop, calls=%fused_computation.7 | loop fusion | bytes 16777216 | tf_op jit(solution)/shard_map/stack | solution.py:9
  22.3 0.0 copy-done.5
  22.3 2.3 convert_bitcast_fusion
  24.7 1.1 copy.44
  25.7 72.6 %all_to_all.30 = bf16[3,8,128,512]{3,2,0,1:T(8,128)(2,1)S(1)} all-to-all(bf16[3,8,128,512]{3,2,0,1:T(8,128)(2,1)S(1)} %copy.44), channel_id=1, replica_groups=mesh['seg'=8,'rep'=4] {'seg'}, dimensions={1} | all-to-all | bytes 6291456 | tf_op jit(solution)/shard_map/all_to_all | solution.py:13
  98.4 1.2 fusion.28
  99.5 0.5 convolution_bitcast_fusion.2
  100.0 0.0 copy-start.3
  100.0 0.5 convolution_bitcast_fusion.3
  100.5 0.3 copy-done.3
  100.8 0.8 copy-done.4
  101.7 0.0 copy-done.6
  101.7 1.4 fusion.11
  103.1 6.0 %copy.51 = bf16[1,1,1024,512]{3,1,0,2:T(2,128)(2,1)} copy(bf16[1,1,1024,512]{2,3,1,0:T(8,128)(2,1)} %fusion.11) | data formatting | bytes 2097152 | tf_op jit(solution)/shard_map/broadcast_in_dim | solution.py:34
  109.1 0.5 broadcast.11
  109.6 9.0 %reduce = bf16[1024,512]{1,0:T(8,128)(2,1)} reduce(bf16[1024,1,1,512]{3,2,1,0:T(2,128)(2,1)} %bitcast.99, bf16[]{:T(256)} %broadcast.11), dimensions={1,2}, to_apply=%bitcast.79.reduce_sub_computation | reduce | bytes 2097154
  118.6 2.6 reshape.33
  121.2 28.8 %all_to_all.31 = bf16[8,2,32768]{2,1,0:T(2,128)(2,1)} all-to-all(bf16[8,2,32768]{2,1,0:T(2,128)(2,1)} %reshape.33), channel_id=1, replica_groups=mesh['seg'=8,'rep'=4] {'seg'}, dimensions={0} | all-to-all | bytes 2097152 | tf_op jit(solution)/shard_map/all_to_all | solution.py:34
  150.0 5.8 %reshape.34 = bf16[1024,1,1,512]{3,2,1,0:T(2,128)(2,1)} reshape(bf16[8,2,32768]{2,1,0:T(2,128)(2,1)} %all_to_all.31) | data formatting | bytes 2097152
  155.8 1.9 copy.59
  157.7 4.7 %convolution_bitcast_fusion.1 = f32[1,32,128,512]{3,1,2,0:T(8,128)} fusion(bf16[8,128,512]{2,1,0:T(8,128)(2,1)S(1)} %bitcast.100, bf16[1,8,32]{2,1,0:T(8,128)(2,1)S(1)} %copy-done.5), kind=kOutput, calls=%fused_computation.10 | convolution fusion | flops 33554432 | bytes 9437696 | tf_op jit(solution)/shard_map/se,ksdh->kedh/dot_general | solution.py:23
  162.4 0.0 reduce-scatter.5.cloned.1.call-update
  162.4 0.0 reduce-scatter.3.cloned.1.call-start
  162.4 2.2 multiply_convert_fusion.1
  164.7 0.4 fusion.10
  165.1 0.4 fusion.9
  165.6 1.5 maximum_bitcast_fusion
  167.1 6.2 %copy.48 = bf16[2,1,1024,512]{3,0,1,2:T(2,128)(2,1)} copy(bf16[2,1,1024,512]{2,3,0,1:T(8,128)(2,1)} %maximum_bitcast_fusion) | data formatting | bytes 4194304 | tf_op jit(solution)/shard_map/broadcast_in_dim | solution.py:53
  173.3 51.5 %all_to_all.32 = bf16[2,1,1024,512]{3,0,1,2:T(2,128)(2,1)S(1)} all-to-all(bf16[2,1,1024,512]{3,0,1,2:T(2,128)(2,1)} %copy.48), channel_id=1, replica_groups=mesh['seg'=8,'rep'=4] {'seg'}, dimensions={2} | all-to-all | bytes 4194304 | tf_op jit(solution)/shard_map/all_to_all | solution.py:54
  224.8 9.1 %convolution_bitcast_fusion = f32[2,32,128,512]{3,1,2,0:T(8,128)} fusion(bf16[2,8,128,512]{3,0,2,1:T(2,128)(2,1)S(1)} %bitcast.97, bf16[1,8,32]{2,1,0:T(8,128)(2,1)S(1)} %copy-done.5), kind=kOutput, calls=%fused_computation.6 | convolution fusion | flops 67108864 | bytes 18874880 | tf_op jit(solution)/shard_map/se,ksdh->kedh/dot_general | solution.py:23
  233.9 0.0 reduce-scatter.3.cloned.1.call-update
  233.9 0.5 fusion.29
  234.4 1.3 fusion.13
  235.7 1.3 reduce-scatter.5.cloned.1.call-done
  237.0 1.7 convert_bitcast_fusion.1
  238.8 1.3 copy.55
  240.1 125.9 %reduce-scatter.3.cloned.1.call-done = f32[2,8,128,512]{3,1,2,0:T(8,128)} async-done(((f32[2,32,128,512]{3,1,2,0:T(8,128)}), f32[2,8,128,512]{3,1,2,0:T(8,128)}) %reduce-scatter.3.cloned.1.call-update) | async-done | bytes 4194320 | tf_op jit(solution)/shard_map/reduce_scatter | solution.py:55
  365.9 2.5 convert.4
  368.4 0.1 slice_bitcast_fusion
  368.5 1.3 copy.54
  369.8 1.3 copy.53
  (4 shorter events, 0.0 us)
Async XLA Ops:
  7.2 92.4 %copy-start = (bf16[1,256,1024]{2,1,0:T(8,128)(2,1)S(1)}, bf16[1,256,1024]{2,1,0:T(8,128)(2,1)}, u32[]{:S(2)}) copy-start(bf16[1,256,1024]{2,1,0:T(8,128)(2,1)} %param.6) | copy-start | bytes 1572868
  7.2 229.9 %reduce-scatter.5.cloned.1.call-start = ((), (), s32[]{:S(2)}) async-start(), calls=%async_computation.6 | async-start | bytes 10485760 | tf_op jit(solution)/shard_map/reduce_scatter | solution.py:36
  7.2 4.7 %copy-start.1 = (bf16[32,128,512]{2,1,0:T(8,128)(2,1)S(1)}, bf16[32,128,512]{2,1,0:T(8,128)(2,1)}, u32[]{:S(2)}) copy-start(bf16[32,128,512]{2,1,0:T(8,128)(2,1)} %param.11) | copy-start | bytes 12582916
  7.2 4.8 %copy-start.2 = (bf16[32,128,512]{2,1,0:T(8,128)(2,1)S(1)}, bf16[32,128,512]{2,1,0:T(8,128)(2,1)}, u32[]{:S(2)}) copy-start(bf16[32,128,512]{2,1,0:T(8,128)(2,1)} %param.10) | copy-start | bytes 12582916
  12.0 10.3 %copy-start.5 = (bf16[1,8,32]{2,1,0:T(8,128)(2,1)S(1)}, bf16[1,8,32]{2,1,0:T(8,128)(2,1)}, u32[]{:S(2)}) copy-start(bf16[1,8,32]{2,1,0:T(8,128)(2,1)} %param.8) | copy-start | bytes 1540
  98.4 3.3 copy-start.6
  100.0 0.8 copy-start.3
  100.8 0.8 copy-start.4
  162.4 203.5 %reduce-scatter.3.cloned.1.call-start = ((), (), s32[]{:S(2)}) async-start(), calls=%async_computation.5 | async-start | bytes 20971520 | tf_op jit(solution)/shard_map/reduce_scatter | solution.py:55
Sparse Core Ops, SparseCore 0:
  162.5 74.4 reduce-scatter.4
  239.8 126.0 reduce-scatter.2
where the time goes:
time: 380 us; the launch traced here: 378 us
  blocking collectives  153 us (40%)
  waiting for transfers between devices  127 us (33%)
  local copies, waits for them, and re-layouts  45.4 us (12%)
  matrix products  23.4 us (6%)
  other arithmetic  14.7 us (4%)
  between operations  14.2 us (4%)
    reduce_scatter x1, waiting for transfers between devices, local(): lax.psum_scatter(pair_folded, 'rep', scatter_dimension=1, tiled=True)  126 us
    all_to_all x1, blocking collectives, local(): lax.all_to_all(merged, 'seg', split_axis=1, concat_axis=2, tiled=True)  72.6 us
    all_to_all x1, blocking collectives, local(): lax.all_to_all(pair, 'seg', split_axis=2, concat_axis=1, tiled=True)  51.5 us
    all_to_all x1, blocking collectives, local(): lax.all_to_all(grad_down_seg[None, None], 'seg', split_axis=2, concat_axi...  28.8 us
    unnamed x22, local copies, waits for them, and re-layouts  20.5 us
    dot_general x2, matrix products, fold_experts(): jnp.einsum('se,ksdh->kedh', mixing, pieces, preferred_element_type=jnp.fl...  13.8 us
    another operation x1, local copies, waits for them, and re-layouts, local(): stacked = jnp.stack([w_gate, w_up, w_down])  10.3 us
    unnamed x1, other arithmetic  9 us
  transfers between devices with their start and end apart: 2, of which 2 were waited for; matrix products, arithmetic and copies ran while one was open for 7% of the time, Pallas kernels for 0%

commit v1 on v0

--- a/solution.py
+++ b/solution.py
@@ -1,7 +1,298 @@
+import functools
+
 import jax
 import jax.numpy as jnp
 from jax import lax
+from jax.experimental import pallas as pl
+from jax.experimental.pallas import tpu as pltpu
 from jax.sharding import PartitionSpec as P
+
+MESH = pl.DeviceIdType.MESH
+F32 = jnp.float32
+BF16 = jnp.bfloat16
+T = 16
+GATE, UP, DOWN = 0, 1, 2
+
+
+def one_hot(shape, rows_of, columns_of):
+    row = lax.broadcasted_iota(jnp.int32, shape, 0)
+    column = lax.broadcasted_iota(jnp.int32, shape, 1)
+    return rows_of(row) == columns_of(column)
+
+
+def dot(a, b):
+    return jnp.dot(a, b, preferred_element_type=F32)
+
+
+def dot_t(a, b):
+    return lax.dot_general(a, b, (((1,), (1,)), ((), ())), preferred_element_type=F32)
+
+
+def kernel(
+    S, R, coef_ref, tok_hbm, cot_hbm, wg_hbm, wu_hbm, wd_hbm,
+    ig_hbm, gg_hbm, gu_hbm, gd_hbm,
+    x, g, xt, gt, w, msend, mfull, gsend, gall, outv, igv, cbuf, mix, fold,
+    gate_s, up_s, dh_s, hid_s, dgate_s, dup_s,
+    load_sem, out_sem, fsend, frecv, bsend, brecv, xsend, xrecv, ssend, srecv, csend, crecv,
+):
+    me = lax.axis_index("seg")
+    rep = lax.axis_index("rep")
+    E, rows, H = w.shape[1:]
+    EL = outv.shape[1]
+    chips = R // 2
+    sibling = rep + 1 - 2 * lax.rem(rep, 2)
+
+    def seg_at(k):
+        return lax.rem(me + k, S)
+
+    def seg_from(k):
+        return lax.rem(me - k + S, S)
+
+    def rep_at(k):
+        return lax.rem(rep + k, R)
+
+    def rep_from(k):
+        return lax.rem(rep - k + R, R)
+
+    def loop(lo, hi, body):
+        lax.fori_loop(lo, hi, lambda i, c: (body(i), c)[1], 0)
+
+    loads = [pltpu.make_async_copy(tok_hbm.at[0], x, load_sem.at[0]),
+             pltpu.make_async_copy(cot_hbm.at[0], g, load_sem.at[1])]
+    w_loads = [pltpu.make_async_copy(h, w.at[p], load_sem.at[2 + p])
+               for p, h in enumerate((wg_hbm, wu_hbm, wd_hbm))]
+    for c in w_loads + loads:
+        c.start()
+
+    barrier = pltpu.get_barrier_semaphore()
+    for k in range(1, S):
+        pl.semaphore_signal(barrier, inc=1, device_id={"seg": seg_at(k)}, device_id_type=MESH)
+    for k in range(1, R):
+        pl.semaphore_signal(barrier, inc=1, device_id={"rep": rep_at(k)}, device_id_type=MESH)
+
+    coef = coef_ref[0].astype(F32)
+    LANES = cbuf.shape[2]
+    cbuf[rep] = dot(coef, one_hot((E, LANES), lambda i: i, lambda j: j).astype(F32))
+    tall = dot(one_hot((S * T, S), lambda i: i // T, lambda j: j).astype(F32), coef)
+    wide = dot(tall, one_hot((E, E * T), lambda i: i, lambda j: j // T).astype(F32))
+    keep = one_hot((S * T, E * T), lambda i: i % T, lambda j: j % T)
+    mix[...] = jnp.where(keep, wide, 0.0).astype(BF16)
+
+    pl.semaphore_wait(barrier, S - 1 + R - 1)
+
+    def coef_copy(k, owner):
+        return pltpu.make_async_remote_copy(
+            src_ref=cbuf.at[owner], dst_ref=cbuf.at[owner],
+            send_sem=csend.at[k], recv_sem=crecv.at[k],
+            device_id={"rep": rep_at(k)}, device_id_type=MESH)
+
+    for k in range(1, R):
+        coef_copy(k, rep).start()
+
+    def merged_copy(p, k, owner):
+        at = pl.ds(pl.multiple_of(owner * rows, rows), rows)
+        return pltpu.make_async_remote_copy(
+            src_ref=msend.at[p, seg_at(k)], dst_ref=mfull.at[p, at],
+            send_sem=fsend.at[p, k], recv_sem=frecv.at[p, k],
+            device_id={"seg": seg_at(k)}, device_id_type=MESH)
+
+    for p in (GATE, UP, DOWN):
+        w_loads[p].wait()
+
+        def merge(b, p=p):
+            at = pl.ds(pl.multiple_of(b * T, T), T)
+            block = dot(mix[...], w[p, :, at, :].reshape(E * T, H))
+            msend[p, :, at, :] = block.astype(BF16).reshape(S, T, H)
+
+        loop(0, rows // T, merge)
+        loop(1, S, lambda k, p=p: merged_copy(p, k, me).start())
+        mfull[p, pl.ds(pl.multiple_of(me * rows, rows), rows), :] = msend[p, me]
+
+    for c in loads:
+        c.wait()
+    xt[...] = x[...].T
+    gt[...] = g[...].T
+    for k in range(1, R):
+        coef_copy(k, rep_from(k)).wait_recv()
+    every = cbuf[...].reshape(R * S, LANES)
+    mine = one_hot((EL * T, LANES), lambda i: i // T + rep * EL, lambda j: j).astype(F32)
+    tall = dot_t(mine, every)
+    wide = dot(tall, one_hot((R * S, R * S * T), lambda i: i, lambda j: j // T).astype(F32))
+    keep = one_hot((EL * T, R * S * T), lambda i: i % T, lambda j: j % T)
+    fold[...] = jnp.where(keep, wide, 0.0).astype(BF16)
+
+    def grad_copy(p, k, owner):
+        return pltpu.make_async_remote_copy(
+            src_ref=gsend.at[p, k], dst_ref=gall.at[p, rep, owner],
+            send_sem=bsend.at[p, k], recv_sem=brecv.at[p, k],
+            device_id={"seg": seg_at(k)}, device_id_type=MESH)
+
+    def chip_copy(p, j, k, owner):
+        block = gall.at[p, owner, seg_from(k)]
+        return pltpu.make_async_remote_copy(
+            src_ref=block, dst_ref=block,
+            send_sem=xsend.at[p, j, k], recv_sem=xrecv.at[p, j, k],
+            device_id={"rep": rep_at(2 * j)}, device_id_type=MESH)
+
+    def sibling_copy(p, j, k, owner):
+        block = gall.at[p, owner, seg_from(k)]
+        return pltpu.make_async_remote_copy(
+            src_ref=block, dst_ref=block,
+            send_sem=ssend.at[p, j, k], recv_sem=srecv.at[p, j, k],
+            device_id={"rep": sibling}, device_id_type=MESH)
+
+    def pass_on(p, k):
+        for j in range(1, chips):
+            chip_copy(p, j, k, rep).start()
+        sibling_copy(p, 0, k, rep).start()
+
+    def send_grads(p, transposed, right):
+        def one(k):
+            at = pl.ds(pl.multiple_of(seg_at(k) * rows, rows), rows)
+            return dot(transposed[at, :], right[...]).astype(BF16)
+
+        def step(k):
+            gsend[p, k] = one(k)
+            grad_copy(p, k, me).start()
+
+        loop(1, S, step)
+        gall[p, rep, me] = one(0)
+        pass_on(p, 0)
+
+    loop(1, S, lambda k: merged_copy(GATE, k, seg_from(k)).wait_recv())
+    gate_s[...] = dot(x[...], mfull[GATE])
+    loop(1, S, lambda k: merged_copy(UP, k, seg_from(k)).wait_recv())
+    up_s[...] = dot(x[...], mfull[UP])
+    CH = 32
+    tokens = x.shape[0]
+
+    def hidden(i):
+        at = pl.ds(pl.multiple_of(i * CH, CH), CH)
+        gate = gate_s[at, :]
+        hid_s[at, :] = (gate * jax.nn.sigmoid(gate) * up_s[at, :]).astype(BF16)
+
+    loop(0, tokens // CH, hidden)
+    send_grads(DOWN, gt, hid_s)
+
+    loop(1, S, lambda k: merged_copy(DOWN, k, seg_from(k)).wait_recv())
+    dh_s[...] = dot(g[...], mfull[DOWN])
+
+    def backward(i):
+        at = pl.ds(pl.multiple_of(i * CH, CH), CH)
+        gate = gate_s[at, :]
+        dh = dh_s[at, :]
+        sigma = jax.nn.sigmoid(gate)
+        dgate_s[at, :] = (dh * up_s[at, :] * sigma * (1.0 + gate * (1.0 - sigma))).astype(BF16)
+        dup_s[at, :] = (dh * (gate * sigma)).astype(BF16)
+
+    loop(0, tokens // CH, backward)
+    send_grads(GATE, xt, dgate_s)
+    send_grads(UP, xt, dup_s)
+
+    def input_grad(i):
+        at = pl.ds(pl.multiple_of(i * rows, rows), rows)
+        total = dot_t(dgate_s[...], mfull[GATE, at, :]) + dot_t(dup_s[...], mfull[UP, at, :])
+        igv[:, at] = total.astype(BF16)
+
+    loop(0, S, input_grad)
+    ig_copy = pltpu.make_async_copy(igv, ig_hbm.at[0], out_sem.at[3])
+    ig_copy.start()
+
+    outs = (gg_hbm, gu_hbm, gd_hbm)
+    out_copies = []
+    for p in (DOWN, GATE, UP):
+        def arrived(k, p=p):
+            grad_copy(p, k, seg_from(k)).wait_recv()
+            pass_on(p, k)
+
+        loop(1, S, arrived)
+
+        def from_chip(k, p=p):
+            for j in range(1, chips):
+                owner = rep_from(2 * j)
+                chip_copy(p, j, k, owner).wait_recv()
+                sibling_copy(p, j, k, owner).start()
+
+        loop(0, S, from_chip)
+
+        def from_sibling(k, p=p):
+            for j in range(chips):
+                sibling_copy(p, j, k, lax.rem(sibling - 2 * j + R, R)).wait_recv()
+
+        loop(0, S, from_sibling)
+
+        def folded(b, p=p):
+            at = pl.ds(pl.multiple_of(b * T, T), T)
+            block = dot(fold[...], gall[p, :, :, at, :].reshape(R * S * T, H))
+            outv[p, :, at, :] = block.astype(BF16).reshape(EL, T, H)
+
+        loop(0, rows // T, folded)
+        c = pltpu.make_async_copy(outv.at[p], outs[p], out_sem.at[p])
+        c.start()
+        out_copies.append(c)
+
+    for k in range(1, R):
+        coef_copy(k, rep).wait_send()
+    for p in (GATE, UP, DOWN):
+        def sent(k, p=p):
+            merged_copy(p, k, me).wait_send()
+            grad_copy(p, k, me).wait_send()
+
+        loop(1, S, sent)
+
+        def passed(k, p=p):
+            for j in range(1, chips):
+                chip_copy(p, j, k, rep).wait_send()
+            for j in range(chips):
+                sibling_copy(p, j, k, rep_from(2 * j)).wait_send()
+
+        loop(0, S, passed)
+    ig_copy.wait()
+    for c in out_copies:
+        c.wait()
+
+
+def fused(S, R, tokens, cotangent, coefficients, w_gate, w_up, w_down):
+    E, rows, H = w_gate.shape
+    L, D = tokens.shape[1:]
+    EL = E // R
+    chips = R // 2
+    lanes = -(-E // 128) * 128
+    any_spec = pl.BlockSpec(memory_space=pl.ANY)
+    dma = pltpu.SemaphoreType.DMA
+    vmem = pltpu.VMEM
+    grad = jax.ShapeDtypeStruct((EL, rows, H), BF16)
+    flops = 16 * L * D * H + 2 * 3 * T * rows * H * E * S + 2 * 3 * T * rows * H * EL * R * S
+    return pl.pallas_call(
+        functools.partial(kernel, S, R),
+        out_shape=(jax.ShapeDtypeStruct((1, L, D), BF16), grad, grad, grad),
+        in_specs=[pl.BlockSpec(memory_space=vmem)] + [any_spec] * 5,
+        out_specs=(any_spec,) * 4,
+        scratch_shapes=[
+            vmem((L, D), BF16), vmem((L, D), BF16), vmem((D, L), BF16), vmem((D, L), BF16),
+            vmem((3, E, rows, H), BF16),
+            vmem((3, S, rows, H), BF16),
+            vmem((3, D, H), BF16),
+            vmem((3, S, rows, H), BF16),
+            vmem((3, R, S, rows, H), BF16),
+            vmem((3, EL, rows, H), BF16),
+            vmem((L, D), BF16),
+            vmem((R, S, lanes), F32),
+            vmem((S * T, E * T), BF16),
+            vmem((EL * T, R * S * T), BF16),
+            vmem((L, H), F32), vmem((L, H), F32), vmem((L, H), F32),
+            vmem((L, H), BF16), vmem((L, H), BF16), vmem((L, H), BF16),
+            dma((5,)), dma((4,)),
+            dma((3, S)), dma((3, S)), dma((3, S)), dma((3, S)),
+            dma((3, chips, S)), dma((3, chips, S)), dma((3, chips, S)), dma((3, chips, S)),
+            dma((R,)), dma((R,)),
+        ],
+        compiler_params=pltpu.CompilerParams(
+            collective_id=0, has_side_effects=True, vmem_limit_bytes=58 * 1024 * 1024),
+        cost_estimate=pl.CostEstimate(
+            flops=flops, bytes_accessed=2 * (3 * E * rows * H + 3 * L * D + 3 * EL * rows * H),
+            transcendentals=2 * L * H),
+    )(coefficients, tokens, cotangent, w_gate, w_up, w_down)
 
 
 def local(tokens, cotangent, coefficients, w_gate, w_up, w_down):
@@ -67,8 +358,16 @@
         P(None, "seg", None),
         P(None, "seg", None),
     )
+    S, R = mesh.shape["seg"], mesh.shape["rep"]
+
+    def body(tokens, cotangent, coefficients, w_gate, w_up, w_down):
+        args = (tokens, cotangent, coefficients, w_gate, w_up, w_down)
+        if w_gate.shape[1] % 128 == 0 and R % 2 == 0 and tokens.shape[1] % 128 == 0:
+            return fused(S, R, *args)
+        return local(*args)
+
     return jax.shard_map(
-        local,
+        body,
         mesh=mesh,
         in_specs=placed,
         out_specs=(

time: 380 us -> 196 us (0.52)
  Pallas kernels: 0 us -> 185 us
  blocking collectives: 153 us -> 0 us
  waiting for transfers between devices: 127 us -> 0 us
  local copies, waits for them, and re-layouts: 45.4 us -> 7.45 us
  matrix products: 23.4 us -> 0 us
  other arithmetic: 14.7 us -> 0 us
  between operations: 14.2 us -> 0.65 us
    pallas_call x0 -> x1, Pallas kernels: none -> 185 us  [fused(): pl.pallas_call(functools.partial(kernel, S, R), out_shape=(jax.ShapeDtype...]
    all_to_all x3 -> x0, blocking collectives: 153 us -> none  [the longest x1 72.6 us: local(): lax.all_to_all(merged, 'seg', split_axis=1, concat_axis=2, tiled=True)]
    reduce_scatter x2 -> x0, waiting for transfers between devices: 127 us -> none  [the longest x1 126 us: local(): lax.psum_scatter(pair_folded, 'rep', scatter_dimension=1, tiled=True)]
    dot_general x11 -> x0, matrix products: 23.4 us -> none  [the longest x2 13.8 us: fold_experts(): jnp.einsum('se,ksdh->kedh', mixing, pieces, preferred_element_type=jnp.fl...]
    unnamed x22 -> x6, local copies, waits for them, and re-layouts: 20.5 us -> 7.45 us
    broadcast_in_dim x2 -> x0, local copies, waits for them, and re-layouts: 12.1 us -> none  [the longest x1 6.19 us: local(): pair = jnp.stack([grad_gate_seg, grad_up_seg])[:, None]]
    another operation x1 -> x0, local copies, waits for them, and re-layouts: 10.3 us -> none  [local(): stacked = jnp.stack([w_gate, w_up, w_down])]
    unnamed x1 -> x0, other arithmetic: 9 us -> none
  transfers between devices with their start and end apart: 2 -> 0, of which waited for: 2 -> 0; matrix products, arithmetic and copies ran while one was open for 7% -> 0% of each run, Pallas kernels for 0% -> 0%
where the time goes in v1:
time: 196 us; the launch traced here: 193 us
  Pallas kernels  185 us (94%)
  local copies, waits for them, and re-layouts  7.45 us (4%)
    pallas_call x1, Pallas kernels, fused(): pl.pallas_call(functools.partial(kernel, S, R), out_shape=(jax.ShapeDtype...  185 us
    unnamed x6, local copies, waits for them, and re-layouts  7.45 us

profile of v1, /device:TPU:21, one launch (start us, length us, event | category | flops | bytes accessed | tf_op | source)
XLA Modules:
  0.0 192.7 jit_solution(14309007899810409817)
XLA Ops:
  0.6 184.6 %shard_map.93 = (bf16[1,256,1024]{2,1,0:T(8,128)(2,1)}, bf16[8,128,512]{2,1,0:T(8,128)(2,1)}, bf16[8,128,512]{2,1,0:T(8,128)(2,1)}, bf16[8,128,512]{2,1,0:T(8,128)(2,1)}) custom-call(bf16[1,8,32]{2,1,0:T(8,128)(2,1)} %coef_ref.1, bf16[1,256,1024]{2,1,0:T(8,128)(2,1)} %tok_hbm.1, bf16[1,256,1024]{2,1,0:T(8,128)(2,1)} %cot_hbm.1, ...), custom_call_target="tpu_custom_call" | custom-call | flops 5368709120 | bytes 17301504 | tf_op jit(solution)/shard_map/pallas_call | solution.py:266
  185.3 0.0 copy-start
  185.3 2.0 %copy.14 = bf16[1,256,1024]{2,1,0:T(8,128)(2,1)} copy(bf16[1,256,1024]{2,1,0:T(8,128)(2,1)} %get-tuple-element.8) | data formatting | bytes 1048576
  187.2 2.3 %copy.15 = bf16[8,128,512]{2,1,0:T(8,128)(2,1)} copy(bf16[8,128,512]{2,1,0:T(8,128)(2,1)} %get-tuple-element.9) | data formatting | bytes 2097152
  189.5 2.3 %copy.16 = bf16[8,128,512]{2,1,0:T(8,128)(2,1)} copy(bf16[8,128,512]{2,1,0:T(8,128)(2,1)} %get-tuple-element.10) | data formatting | bytes 2097152
  191.8 0.0 copy-done
  191.8 1.0 copy.17
Async XLA Ops:
  185.3 6.5 %copy-start = (bf16[8,128,512]{2,1,0:T(8,128)(2,1)S(1)}, bf16[8,128,512]{2,1,0:T(8,128)(2,1)}, u32[]{:S(2)}) copy-start(bf16[8,128,512]{2,1,0:T(8,128)(2,1)} %get-tuple-element.11) | copy-start | bytes 3145732

commit v2 on v1

--- a/solution.py
+++ b/solution.py
@@ -105,7 +105,8 @@
             msend[p, :, at, :] = block.astype(BF16).reshape(S, T, H)
 
         loop(0, rows // T, merge)
-        loop(1, S, lambda k, p=p: merged_copy(p, k, me).start())
+        if p == GATE:
+            loop(1, S, lambda k: merged_copy(GATE, k, me).start())
         mfull[p, pl.ds(pl.multiple_of(me * rows, rows), rows), :] = msend[p, me]
 
     for c in loads:
@@ -121,46 +122,60 @@
     keep = one_hot((EL * T, R * S * T), lambda i: i % T, lambda j: j % T)
     fold[...] = jnp.where(keep, wide, 0.0).astype(BF16)
 
-    def grad_copy(p, k, owner):
+    def send_after(p, before):
+        def step(k):
+            merged_copy(before, k, me).wait_send()
+            merged_copy(p, k, me).start()
+
+        loop(1, S, step)
+
+    Q = bsend.shape[1]
+    part = rows // Q
+
+    def piece(c):
+        return pl.ds(c * part, part)
+
+    def grad_copy(p, c, k, owner):
         return pltpu.make_async_remote_copy(
-            src_ref=gsend.at[p, k], dst_ref=gall.at[p, rep, owner],
-            send_sem=bsend.at[p, k], recv_sem=brecv.at[p, k],
+            src_ref=gsend.at[p, k, piece(c)], dst_ref=gall.at[p, rep, owner, piece(c)],
+            send_sem=bsend.at[p, c, k], recv_sem=brecv.at[p, c, k],
             device_id={"seg": seg_at(k)}, device_id_type=MESH)
 
-    def chip_copy(p, j, k, owner):
-        block = gall.at[p, owner, seg_from(k)]
+    def chip_copy(p, c, j, owner):
+        block = gall.at[p, owner, :, piece(c)]
         return pltpu.make_async_remote_copy(
             src_ref=block, dst_ref=block,
-            send_sem=xsend.at[p, j, k], recv_sem=xrecv.at[p, j, k],
+            send_sem=xsend.at[p, c, j], recv_sem=xrecv.at[p, c, j],
             device_id={"rep": rep_at(2 * j)}, device_id_type=MESH)
 
-    def sibling_copy(p, j, k, owner):
-        block = gall.at[p, owner, seg_from(k)]
+    def sibling_copy(p, c, j, owner):
+        block = gall.at[p, owner, :, piece(c)]
         return pltpu.make_async_remote_copy(
             src_ref=block, dst_ref=block,
-            send_sem=ssend.at[p, j, k], recv_sem=srecv.at[p, j, k],
+            send_sem=ssend.at[p, c, j], recv_sem=srecv.at[p, c, j],
             device_id={"rep": sibling}, device_id_type=MESH)
 
-    def pass_on(p, k):
-        for j in range(1, chips):
-            chip_copy(p, j, k, rep).start()
-        sibling_copy(p, 0, k, rep).start()
-
-    def send_grads(p, transposed, right):
+    def make_grads(p, transposed, right):
         def one(k):
             at = pl.ds(pl.multiple_of(seg_at(k) * rows, rows), rows)
             return dot(transposed[at, :], right[...]).astype(BF16)
 
         def step(k):
             gsend[p, k] = one(k)
-            grad_copy(p, k, me).start()
 
         loop(1, S, step)
         gall[p, rep, me] = one(0)
-        pass_on(p, 0)
-
+
+    def send(p, c):
+        loop(1, S, lambda k: grad_copy(p, c, k, me).start())
+
+    def sent(p, c):
+        loop(1, S, lambda k: grad_copy(p, c, k, me).wait_send())
+
+    send_after(UP, GATE)
     loop(1, S, lambda k: merged_copy(GATE, k, seg_from(k)).wait_recv())
     gate_s[...] = dot(x[...], mfull[GATE])
+    send_after(DOWN, UP)
     loop(1, S, lambda k: merged_copy(UP, k, seg_from(k)).wait_recv())
     up_s[...] = dot(x[...], mfull[UP])
     CH = 32
@@ -172,7 +187,12 @@
         hid_s[at, :] = (gate * jax.nn.sigmoid(gate) * up_s[at, :]).astype(BF16)
 
     loop(0, tokens // CH, hidden)
-    send_grads(DOWN, gt, hid_s)
+    make_grads(DOWN, gt, hid_s)
+    loop(1, S, lambda k: merged_copy(DOWN, k, me).wait_send())
+    steps = [(p, c) for p in (DOWN, GATE, UP) for c in range(Q)]
+    AHEAD = 2
+    for p, c in steps[:AHEAD]:
+        send(p, c)
 
     loop(1, S, lambda k: merged_copy(DOWN, k, seg_from(k)).wait_recv())
     dh_s[...] = dot(g[...], mfull[DOWN])
@@ -186,70 +206,95 @@
         dup_s[at, :] = (dh * (gate * sigma)).astype(BF16)
 
     loop(0, tokens // CH, backward)
-    send_grads(GATE, xt, dgate_s)
-    send_grads(UP, xt, dup_s)
 
     def input_grad(i):
         at = pl.ds(pl.multiple_of(i * rows, rows), rows)
         total = dot_t(dgate_s[...], mfull[GATE, at, :]) + dot_t(dup_s[...], mfull[UP, at, :])
         igv[:, at] = total.astype(BF16)
 
-    loop(0, S, input_grad)
     ig_copy = pltpu.make_async_copy(igv, ig_hbm.at[0], out_sem.at[3])
-    ig_copy.start()
-
     outs = (gg_hbm, gu_hbm, gd_hbm)
-    out_copies = []
-    for p in (DOWN, GATE, UP):
-        def arrived(k, p=p):
-            grad_copy(p, k, seg_from(k)).wait_recv()
-            pass_on(p, k)
-
-        loop(1, S, arrived)
-
-        def from_chip(k, p=p):
+    out_copies = [ig_copy]
+    for i in range(AHEAD, len(steps) + 4):
+        if i < len(steps):
+            sent(*steps[i - AHEAD])
+            send(*steps[i])
+        if i == AHEAD:
+            make_grads(GATE, xt, dgate_s)
+        if i == Q:
+            make_grads(UP, xt, dup_s)
+        if i == Q + 1:
+            loop(0, S, input_grad)
+            ig_copy.start()
+        if i - 2 < len(steps):
+            p, c = steps[i - 2]
+
+            def arrived(k, p=p, c=c):
+                grad_copy(p, c, k, seg_from(k)).wait_recv()
+
+            loop(1, S, arrived)
             for j in range(1, chips):
-                owner = rep_from(2 * j)
-                chip_copy(p, j, k, owner).wait_recv()
-                sibling_copy(p, j, k, owner).start()
-
-        loop(0, S, from_chip)
-
-        def from_sibling(k, p=p):
+                chip_copy(p, c, j, rep).start()
+            sibling_copy(p, c, 0, rep).start()
+        if 0 <= i - 3 < len(steps):
+            p, c = steps[i - 3]
+            for j in range(1, chips):
+                chip_copy(p, c, j, rep_from(2 * j)).wait_recv()
+                sibling_copy(p, c, j, rep_from(2 * j)).start()
+        if 0 <= i - 4 < len(steps):
+            p, c = steps[i - 4]
             for j in range(chips):
-                sibling_copy(p, j, k, lax.rem(sibling - 2 * j + R, R)).wait_recv()
-
-        loop(0, S, from_sibling)
-
-        def folded(b, p=p):
-            at = pl.ds(pl.multiple_of(b * T, T), T)
-            block = dot(fold[...], gall[p, :, :, at, :].reshape(R * S * T, H))
-            outv[p, :, at, :] = block.astype(BF16).reshape(EL, T, H)
-
-        loop(0, rows // T, folded)
-        c = pltpu.make_async_copy(outv.at[p], outs[p], out_sem.at[p])
-        c.start()
-        out_copies.append(c)
+                sibling_copy(p, c, j, lax.rem(sibling - 2 * j + R, R)).wait_recv()
+
+            def folded(b, p=p, c=c):
+                at = pl.ds(pl.multiple_of(c * part + b * T, T), T)
+                block = dot(fold[...], gall[p, :, :, at, :].reshape(R * S * T, H))
+                outv[p, :, at, :] = block.astype(BF16).reshape(EL, T, H)
+
+            loop(0, part // T, folded)
+            if c == Q - 1:
+                out = pltpu.make_async_copy(outv.at[p], outs[p], out_sem.at[p])
+                out.start()
+                out_copies.append(out)
 
     for k in range(1, R):
         coef_copy(k, rep).wait_send()
-    for p in (GATE, UP, DOWN):
-        def sent(k, p=p):
-            merged_copy(p, k, me).wait_send()
-            grad_copy(p, k, me).wait_send()
-
-        loop(1, S, sent)
-
-        def passed(k, p=p):
-            for j in range(1, chips):
-                chip_copy(p, j, k, rep).wait_send()
-            for j in range(chips):
-                sibling_copy(p, j, k, rep_from(2 * j)).wait_send()
-
-        loop(0, S, passed)
-    ig_copy.wait()
-    for c in out_copies:
+    for p, c in steps[-AHEAD:]:
+        sent(p, c)
+    for p, c in steps:
+        for j in range(1, chips):
+            chip_copy(p, c, j, rep).wait_send()
+        for j in range(chips):
+            sibling_copy(p, c, j, rep_from(2 * j)).wait_send()
+    for out in out_copies:
+        out.wait()
+
+
+def place_kernel(n, *refs):
+    sources, targets, held, sems = refs[:n], refs[n:2 * n], refs[2 * n:3 * n], refs[3 * n]
+    loads = [pltpu.make_async_copy(a, b, sems.at[0, i]) for i, (a, b) in enumerate(zip(sources, held))]
+    stores = [pltpu.make_async_copy(a, b, sems.at[1, i]) for i, (a, b) in enumerate(zip(held, targets))]
+    for c in loads:
+        c.start()
+    for a, b in zip(loads, stores):
+        a.wait()
+        b.start()
+    for c in stores:
         c.wait()
+
+
+def place(arrays):
+    n = len(arrays)
+    any_spec = pl.BlockSpec(memory_space=pl.ANY)
+    return pl.pallas_call(
+        functools.partial(place_kernel, n),
+        out_shape=tuple(jax.ShapeDtypeStruct(a.shape, a.dtype) for a in arrays),
+        in_specs=[any_spec] * n,
+        out_specs=(any_spec,) * n,
+        scratch_shapes=[pltpu.VMEM(a.shape, a.dtype) for a in arrays] + [pltpu.SemaphoreType.DMA((2, n))],
+        compiler_params=pltpu.CompilerParams(vmem_limit_bytes=58 * 1024 * 1024),
+        cost_estimate=pl.CostEstimate(flops=0, bytes_accessed=4 * sum(a.size for a in arrays), transcendentals=0),
+    )(*arrays)
 
 
 def fused(S, R, tokens, cotangent, coefficients, w_gate, w_up, w_down):
@@ -263,7 +308,8 @@
     vmem = pltpu.VMEM
     grad = jax.ShapeDtypeStruct((EL, rows, H), BF16)
     flops = 16 * L * D * H + 2 * 3 * T * rows * H * E * S + 2 * 3 * T * rows * H * EL * R * S
-    return pl.pallas_call(
+    Q = 4
+    made = pl.pallas_call(
         functools.partial(kernel, S, R),
         out_shape=(jax.ShapeDtypeStruct((1, L, D), BF16), grad, grad, grad),
         in_specs=[pl.BlockSpec(memory_space=vmem)] + [any_spec] * 5,
@@ -283,8 +329,8 @@
             vmem((L, H), F32), vmem((L, H), F32), vmem((L, H), F32),
             vmem((L, H), BF16), vmem((L, H), BF16), vmem((L, H), BF16),
             dma((5,)), dma((4,)),
-            dma((3, S)), dma((3, S)), dma((3, S)), dma((3, S)),
-            dma((3, chips, S)), dma((3, chips, S)), dma((3, chips, S)), dma((3, chips, S)),
+            dma((3, S)), dma((3, S)), dma((3, Q, S)), dma((3, Q, S)),
+            dma((3, Q, chips)), dma((3, Q, chips)), dma((3, Q, chips)), dma((3, Q, chips)),
             dma((R,)), dma((R,)),
         ],
         compiler_params=pltpu.CompilerParams(
@@ -293,6 +339,7 @@
             flops=flops, bytes_accessed=2 * (3 * E * rows * H + 3 * L * D + 3 * EL * rows * H),
             transcendentals=2 * L * H),
     )(coefficients, tokens, cotangent, w_gate, w_up, w_down)
+    return place(made)
 
 
 def local(tokens, cotangent, coefficients, w_gate, w_up, w_down):

time: 196 us -> 166 us (0.85)
  Pallas kernels: 185 us -> 162 us
  local copies, waits for them, and re-layouts: 7.45 us -> 0 us
    pallas_call x1, Pallas kernels: 185 us -> 159 us  [fused(): pl.pallas_call(functools.partial(kernel, S, R), out_shape=(jax.ShapeDtype...]
    unnamed x6 -> x0, local copies, waits for them, and re-layouts: 7.45 us -> none
    pallas_call x0 -> x1, Pallas kernels: none -> 3.18 us  [place(): pl.pallas_call(functools.partial(place_kernel, n), out_shape=tuple((jax.S...]
where the time goes in v2:
time: 166 us; the launch traced here: 163 us
  Pallas kernels  162 us (98%)
    pallas_call x1, Pallas kernels, fused(): pl.pallas_call(functools.partial(kernel, S, R), out_shape=(jax.ShapeDtype...  159 us

profile of v2, /device:TPU:21, one launch (start us, length us, event | category | flops | bytes accessed | tf_op | source)
XLA Modules:
  0.0 163.0 jit_solution(15682683552832791173)
XLA Ops:
  0.6 159.2 %shard_map.93 = (bf16[1,256,1024]{2,1,0:T(8,128)(2,1)}, bf16[8,128,512]{2,1,0:T(8,128)(2,1)}, bf16[8,128,512]{2,1,0:T(8,128)(2,1)}, bf16[8,128,512]{2,1,0:T(8,128)(2,1)}) custom-call(bf16[1,8,32]{2,1,0:T(8,128)(2,1)} %coef_ref.1, bf16[1,256,1024]{2,1,0:T(8,128)(2,1)} %tok_hbm.1, bf16[1,256,1024]{2,1,0:T(8,128)(2,1)} %cot_hbm.1, ...), custom_call_target="tpu_custom_call" | custom-call | flops 5368709120 | bytes 17301504 | tf_op jit(solution)/shard_map/pallas_call | solution.py:312
  159.8 3.2 %shard_map.94 = (bf16[1,256,1024]{2,1,0:T(8,128)(2,1)}, bf16[8,128,512]{2,1,0:T(8,128)(2,1)}, bf16[8,128,512]{2,1,0:T(8,128)(2,1)}, bf16[8,128,512]{2,1,0:T(8,128)(2,1)}) custom-call(bf16[1,256,1024]{2,1,0:T(8,128)(2,1)} %get-tuple-element.8.refs_0_, bf16[8,128,512]{2,1,0:T(8,128)(2,1)} %get-tuple-element.9.refs_1_, ...), custom_call_target="tpu_custom_call" | custom-call | bytes 7340032 | tf_op jit(solution)/shard_map/pallas_call | solution.py:289

commit v3 on v2

--- a/solution.py
+++ b/solution.py
@@ -29,18 +29,25 @@
 
 
 def kernel(
-    S, R, coef_ref, tok_hbm, cot_hbm, wg_hbm, wu_hbm, wd_hbm,
+    S, R, Q, coef_ref, tok_hbm, cot_hbm, wg_hbm, wu_hbm, wd_hbm,
     ig_hbm, gg_hbm, gu_hbm, gd_hbm,
-    x, g, xt, gt, w, msend, mfull, gsend, gall, outv, igv, cbuf, mix, fold,
-    gate_s, up_s, dh_s, hid_s, dgate_s, dup_s,
-    load_sem, out_sem, fsend, frecv, bsend, brecv, xsend, xrecv, ssend, srecv, csend, crecv,
+    x, g, xt, gt, xp, gp, xpt, gpt, w, msend, mfull, mdown, gown, ghelp, gall, outv, igv, cbuf, mix, fold,
+    gate_s, up_s, dh_s, dhp_s, dhr, d_s, dr,
+    load_sem, out_sem, fsend, frecv, dsend, drecv, psend, precv,
+    osend, orecv, hsend, hrecv, xsend, xrecv, ssend, srecv, csend, crecv,
 ):
     me = lax.axis_index("seg")
     rep = lax.axis_index("rep")
     E, rows, H = w.shape[1:]
     EL = outv.shape[1]
+    L = x.shape[0]
     chips = R // 2
     sibling = rep + 1 - 2 * lax.rem(rep, 2)
+    HS = S // 2
+    place = lax.rem(me, HS)
+    base = me - place
+    other = HS - base
+    partner = other + place
 
     def seg_at(k):
         return lax.rem(me + k, S)
@@ -48,6 +55,12 @@
     def seg_from(k):
         return lax.rem(me - k + S, S)
 
+    def place_at(k):
+        return lax.rem(place + k, HS)
+
+    def place_from(k):
+        return lax.rem(place - k + HS, HS)
+
     def rep_at(k):
         return lax.rem(rep + k, R)
 
@@ -56,6 +69,9 @@
 
     def loop(lo, hi, body):
         lax.fori_loop(lo, hi, lambda i, c: (body(i), c)[1], 0)
+
+    def span(start, count=1):
+        return pl.ds(pl.multiple_of(start * rows, rows), count * rows)
 
     loads = [pltpu.make_async_copy(tok_hbm.at[0], x, load_sem.at[0]),
              pltpu.make_async_copy(cot_hbm.at[0], g, load_sem.at[1])]
@@ -90,11 +106,27 @@
         coef_copy(k, rep).start()
 
     def merged_copy(p, k, owner):
-        at = pl.ds(pl.multiple_of(owner * rows, rows), rows)
-        return pltpu.make_async_remote_copy(
-            src_ref=msend.at[p, seg_at(k)], dst_ref=mfull.at[p, at],
+        return pltpu.make_async_remote_copy(
+            src_ref=msend.at[p, seg_at(k)], dst_ref=mfull.at[p, span(owner)],
             send_sem=fsend.at[p, k], recv_sem=frecv.at[p, k],
             device_id={"seg": seg_at(k)}, device_id_type=MESH)
+
+    def down_copy(t, k, owner):
+        to = place_at(k)
+        return pltpu.make_async_remote_copy(
+            src_ref=msend.at[DOWN, (base if t == 0 else other) + to], dst_ref=mdown.at[t, span(owner)],
+            send_sem=dsend.at[t, k], recv_sem=drecv.at[t, k],
+            device_id={"seg": base + to}, device_id_type=MESH)
+
+    def to_partner(n, source, target):
+        return pltpu.make_async_remote_copy(
+            src_ref=source, dst_ref=target, send_sem=psend.at[n], recv_sem=precv.at[n],
+            device_id={"seg": partner}, device_id_type=MESH)
+
+    x_out = to_partner(0, x.at[:, span(other, HS)], xp)
+    g_out = to_partner(1, g.at[:, span(other, HS)], gp)
+    dh_out = to_partner(2, dhp_s, dhr)
+    d_out = [to_partner(3 + p, d_s.at[p], dr.at[p]) for p in (GATE, UP, DOWN)]
 
     for p in (GATE, UP, DOWN):
         w_loads[p].wait()
@@ -107,12 +139,19 @@
         loop(0, rows // T, merge)
         if p == GATE:
             loop(1, S, lambda k: merged_copy(GATE, k, me).start())
-        mfull[p, pl.ds(pl.multiple_of(me * rows, rows), rows), :] = msend[p, me]
+        if p == DOWN:
+            for k in range(1, HS):
+                for t in range(2):
+                    down_copy(t, k, place).start()
+            mdown[0, span(place), :] = msend[DOWN, me]
+            mdown[1, span(place), :] = msend[DOWN, partner]
+        else:
+            mfull[p, span(me), :] = msend[p, me]
 
     for c in loads:
         c.wait()
-    xt[...] = x[...].T
-    gt[...] = g[...].T
+    xt[...] = x[:, span(base, HS)].T
+    gt[...] = g[:, span(base, HS)].T
     for k in range(1, R):
         coef_copy(k, rep_from(k)).wait_recv()
     every = cbuf[...].reshape(R * S, LANES)
@@ -122,152 +161,217 @@
     keep = one_hot((EL * T, R * S * T), lambda i: i % T, lambda j: j % T)
     fold[...] = jnp.where(keep, wide, 0.0).astype(BF16)
 
-    def send_after(p, before):
-        def step(k):
-            merged_copy(before, k, me).wait_send()
-            merged_copy(p, k, me).start()
-
-        loop(1, S, step)
-
-    Q = bsend.shape[1]
     part = rows // Q
 
     def piece(c):
         return pl.ds(c * part, part)
 
-    def grad_copy(p, c, k, owner):
-        return pltpu.make_async_remote_copy(
-            src_ref=gsend.at[p, k, piece(c)], dst_ref=gall.at[p, rep, owner, piece(c)],
-            send_sem=bsend.at[p, c, k], recv_sem=brecv.at[p, c, k],
-            device_id={"seg": seg_at(k)}, device_id_type=MESH)
+    def own_copy(p, k, owner):
+        return pltpu.make_async_remote_copy(
+            src_ref=gown.at[p, k], dst_ref=gall.at[p, rep, base + owner],
+            send_sem=osend.at[p, k], recv_sem=orecv.at[p, k],
+            device_id={"seg": base + place_at(k)}, device_id_type=MESH)
+
+    def help_copy(p, c, k, owner):
+        return pltpu.make_async_remote_copy(
+            src_ref=ghelp.at[p, k, piece(c)], dst_ref=gall.at[p, rep, other + owner, piece(c)],
+            send_sem=hsend.at[p, c, k], recv_sem=hrecv.at[p, c, k],
+            device_id={"seg": base + place_at(k)}, device_id_type=MESH)
+
+    def unit(p, c, owner):
+        if c == Q:
+            return gall.at[p, owner, pl.ds(base, HS)]
+        return gall.at[p, owner, pl.ds(other, HS), piece(c)]
 
     def chip_copy(p, c, j, owner):
-        block = gall.at[p, owner, :, piece(c)]
+        block = unit(p, c, owner)
         return pltpu.make_async_remote_copy(
             src_ref=block, dst_ref=block,
             send_sem=xsend.at[p, c, j], recv_sem=xrecv.at[p, c, j],
             device_id={"rep": rep_at(2 * j)}, device_id_type=MESH)
 
     def sibling_copy(p, c, j, owner):
-        block = gall.at[p, owner, :, piece(c)]
+        block = unit(p, c, owner)
         return pltpu.make_async_remote_copy(
             src_ref=block, dst_ref=block,
             send_sem=ssend.at[p, c, j], recv_sem=srecv.at[p, c, j],
             device_id={"rep": sibling}, device_id_type=MESH)
 
-    def make_grads(p, transposed, right):
+    def make_own(p):
+        transposed = gt if p == DOWN else xt
+
         def one(k):
-            at = pl.ds(pl.multiple_of(seg_at(k) * rows, rows), rows)
-            return dot(transposed[at, :], right[...]).astype(BF16)
+            return dot(transposed[span(place_at(k)), :], d_s[p]).astype(BF16)
 
         def step(k):
-            gsend[p, k] = one(k)
-
-        loop(1, S, step)
+            gown[p, k] = one(k)
+            own_copy(p, k, place).start()
+
+        loop(1, HS, step)
         gall[p, rep, me] = one(0)
 
-    def send(p, c):
-        loop(1, S, lambda k: grad_copy(p, c, k, me).start())
-
-    def sent(p, c):
-        loop(1, S, lambda k: grad_copy(p, c, k, me).wait_send())
-
-    send_after(UP, GATE)
+    def make_help(p):
+        transposed = gpt if p == DOWN else xpt
+
+        def one(k):
+            return dot(transposed[span(place_at(k)), :], dr[p]).astype(BF16)
+
+        def step(k):
+            ghelp[p, k] = one(k)
+
+        loop(1, HS, step)
+        gall[p, rep, partner] = one(0)
+        for c in range(Q):
+            loop(1, HS, lambda k, c=c: help_copy(p, c, k, place).start())
+
+    def pass_on(p, c):
+        def arrived(k):
+            if c == Q:
+                own_copy(p, k, place_from(k)).wait_recv()
+            else:
+                help_copy(p, c, k, place_from(k)).wait_recv()
+
+        loop(1, HS, arrived)
+        for j in range(1, chips):
+            chip_copy(p, c, j, rep).start()
+        sibling_copy(p, c, 0, rep).start()
+
+    def hand_over(p, c):
+        for j in range(1, chips):
+            chip_copy(p, c, j, rep_from(2 * j)).wait_recv()
+            sibling_copy(p, c, j, rep_from(2 * j)).start()
+
+    def collect(p, c):
+        for j in range(chips):
+            sibling_copy(p, c, j, lax.rem(sibling - 2 * j + R, R)).wait_recv()
+
+    def fold_piece(p, c):
+        collect(p, c)
+
+        def folded(b):
+            at = pl.ds(pl.multiple_of(c * part + b * T, T), T)
+            block = dot(fold[...], gall[p, :, :, at, :].reshape(R * S * T, H))
+            outv[p, :, at, :] = block.astype(BF16).reshape(EL, T, H)
+
+        loop(0, part // T, folded)
+
+    outs = (gg_hbm, gu_hbm, gd_hbm)
+    out_copies = [pltpu.make_async_copy(outv.at[p], outs[p], out_sem.at[p]) for p in (GATE, UP, DOWN)]
+    ig_copy = pltpu.make_async_copy(igv, ig_hbm.at[0], out_sem.at[3])
+
+    def send_up(k):
+        merged_copy(GATE, k, me).wait_send()
+        merged_copy(UP, k, me).start()
+
+    loop(1, S, send_up)
+    g_out.start()
     loop(1, S, lambda k: merged_copy(GATE, k, seg_from(k)).wait_recv())
     gate_s[...] = dot(x[...], mfull[GATE])
-    send_after(DOWN, UP)
+    for k in range(1, HS):
+        for t in range(2):
+            down_copy(t, k, place_from(k)).wait_recv()
+    dh_s[...] = dot(g[:, span(base, HS)], mdown[0])
+
     loop(1, S, lambda k: merged_copy(UP, k, seg_from(k)).wait_recv())
     up_s[...] = dot(x[...], mfull[UP])
     CH = 32
-    tokens = x.shape[0]
+
+    def chunk(i):
+        return pl.ds(pl.multiple_of(i * CH, CH), CH)
 
     def hidden(i):
-        at = pl.ds(pl.multiple_of(i * CH, CH), CH)
+        at = chunk(i)
         gate = gate_s[at, :]
-        hid_s[at, :] = (gate * jax.nn.sigmoid(gate) * up_s[at, :]).astype(BF16)
-
-    loop(0, tokens // CH, hidden)
-    make_grads(DOWN, gt, hid_s)
-    loop(1, S, lambda k: merged_copy(DOWN, k, me).wait_send())
-    steps = [(p, c) for p in (DOWN, GATE, UP) for c in range(Q)]
-    AHEAD = 2
-    for p, c in steps[:AHEAD]:
-        send(p, c)
-
-    loop(1, S, lambda k: merged_copy(DOWN, k, seg_from(k)).wait_recv())
-    dh_s[...] = dot(g[...], mfull[DOWN])
+        d_s[DOWN, at, :] = (gate * jax.nn.sigmoid(gate) * up_s[at, :]).astype(BF16)
+
+    loop(0, L // CH, hidden)
+    d_out[DOWN].start()
+    make_own(DOWN)
+    g_out.wait_recv()
+    dhp_s[...] = dot(gp[...], mdown[1]).astype(BF16)
+    dh_out.start()
+    gpt[...] = gp[...].T
+    x_out.start()
+    pass_on(DOWN, Q)
+    d_out[DOWN].wait_recv()
+    make_help(DOWN)
+
+    dh_out.wait_recv()
 
     def backward(i):
-        at = pl.ds(pl.multiple_of(i * CH, CH), CH)
+        at = chunk(i)
         gate = gate_s[at, :]
-        dh = dh_s[at, :]
+        dh = dh_s[at, :] + dhr[at, :].astype(F32)
         sigma = jax.nn.sigmoid(gate)
-        dgate_s[at, :] = (dh * up_s[at, :] * sigma * (1.0 + gate * (1.0 - sigma))).astype(BF16)
-        dup_s[at, :] = (dh * (gate * sigma)).astype(BF16)
-
-    loop(0, tokens // CH, backward)
+        d_s[GATE, at, :] = (dh * up_s[at, :] * sigma * (1.0 + gate * (1.0 - sigma))).astype(BF16)
+        d_s[UP, at, :] = (dh * (gate * sigma)).astype(BF16)
+
+    loop(0, L // CH, backward)
+    d_out[GATE].start()
+    make_own(GATE)
+    make_own(UP)
+    for c in range(Q):
+        pass_on(DOWN, c)
+    x_out.wait_recv()
+    xpt[...] = xp[...].T
+    d_out[GATE].wait_send()
+    d_out[UP].start()
+    pass_on(GATE, Q)
+    hand_over(DOWN, Q)
 
     def input_grad(i):
-        at = pl.ds(pl.multiple_of(i * rows, rows), rows)
-        total = dot_t(dgate_s[...], mfull[GATE, at, :]) + dot_t(dup_s[...], mfull[UP, at, :])
+        at = span(i)
+        total = dot_t(d_s[GATE], mfull[GATE, at, :]) + dot_t(d_s[UP], mfull[UP, at, :])
         igv[:, at] = total.astype(BF16)
 
-    ig_copy = pltpu.make_async_copy(igv, ig_hbm.at[0], out_sem.at[3])
-    outs = (gg_hbm, gu_hbm, gd_hbm)
-    out_copies = [ig_copy]
-    for i in range(AHEAD, len(steps) + 4):
-        if i < len(steps):
-            sent(*steps[i - AHEAD])
-            send(*steps[i])
-        if i == AHEAD:
-            make_grads(GATE, xt, dgate_s)
-        if i == Q:
-            make_grads(UP, xt, dup_s)
-        if i == Q + 1:
-            loop(0, S, input_grad)
-            ig_copy.start()
-        if i - 2 < len(steps):
-            p, c = steps[i - 2]
-
-            def arrived(k, p=p, c=c):
-                grad_copy(p, c, k, seg_from(k)).wait_recv()
-
-            loop(1, S, arrived)
-            for j in range(1, chips):
-                chip_copy(p, c, j, rep).start()
-            sibling_copy(p, c, 0, rep).start()
-        if 0 <= i - 3 < len(steps):
-            p, c = steps[i - 3]
-            for j in range(1, chips):
-                chip_copy(p, c, j, rep_from(2 * j)).wait_recv()
-                sibling_copy(p, c, j, rep_from(2 * j)).start()
-        if 0 <= i - 4 < len(steps):
-            p, c = steps[i - 4]
-            for j in range(chips):
-                sibling_copy(p, c, j, lax.rem(sibling - 2 * j + R, R)).wait_recv()
-
-            def folded(b, p=p, c=c):
-                at = pl.ds(pl.multiple_of(c * part + b * T, T), T)
-                block = dot(fold[...], gall[p, :, :, at, :].reshape(R * S * T, H))
-                outv[p, :, at, :] = block.astype(BF16).reshape(EL, T, H)
-
-            loop(0, part // T, folded)
-            if c == Q - 1:
-                out = pltpu.make_async_copy(outv.at[p], outs[p], out_sem.at[p])
-                out.start()
-                out_copies.append(out)
+    loop(0, S, input_grad)
+    ig_copy.start()
+    pass_on(UP, Q)
+    d_out[GATE].wait_recv()
+    make_help(GATE)
+    collect(DOWN, Q)
+    for c in range(Q):
+        hand_over(DOWN, c)
+    for c in range(Q):
+        pass_on(GATE, c)
+    for c in range(Q):
+        fold_piece(DOWN, c)
+    out_copies[DOWN].start()
+    d_out[UP].wait_recv()
+    make_help(UP)
+    hand_over(GATE, Q)
+    hand_over(UP, Q)
+    for c in range(Q):
+        pass_on(UP, c)
+    for p in (GATE, UP):
+        collect(p, Q)
+        for c in range(Q + 1):
+            if c < Q:
+                hand_over(p, c)
+            if c > 0:
+                fold_piece(p, c - 1)
+        out_copies[p].start()
 
     for k in range(1, R):
         coef_copy(k, rep).wait_send()
-    for p, c in steps[-AHEAD:]:
-        sent(p, c)
-    for p, c in steps:
-        for j in range(1, chips):
-            chip_copy(p, c, j, rep).wait_send()
-        for j in range(chips):
-            sibling_copy(p, c, j, rep_from(2 * j)).wait_send()
-    for out in out_copies:
-        out.wait()
+    loop(1, S, lambda k: merged_copy(UP, k, me).wait_send())
+    for c in (x_out, g_out, dh_out, d_out[UP], d_out[DOWN]):
+        c.wait_send()
+    for k in range(1, HS):
+        for t in range(2):
+            down_copy(t, k, place).wait_send()
+    for p in (GATE, UP, DOWN):
+        loop(1, HS, lambda k, p=p: own_copy(p, k, place).wait_send())
+        for c in range(Q):
+            loop(1, HS, lambda k, p=p, c=c: help_copy(p, c, k, place).wait_send())
+        for c in range(Q + 1):
+            for j in range(1, chips):
+                chip_copy(p, c, j, rep).wait_send()
+            for j in range(chips):
+                sibling_copy(p, c, j, rep_from(2 * j)).wait_send()
+    ig_copy.wait()
+    for c in out_copies:
+        c.wait()
 
 
 def place_kernel(n, *refs):
@@ -310,16 +414,18 @@
     flops = 16 * L * D * H + 2 * 3 * T * rows * H * E * S + 2 * 3 * T * rows * H * EL * R * S
     Q = 4
     made = pl.pallas_call(
-        functools.partial(kernel, S, R),
+        functools.partial(kernel, S, R, Q),
         out_shape=(jax.ShapeDtypeStruct((1, L, D), BF16), grad, grad, grad),
         in_specs=[pl.BlockSpec(memory_space=vmem)] + [any_spec] * 5,
         out_specs=(any_spec,) * 4,
         scratch_shapes=[
-            vmem((L, D), BF16), vmem((L, D), BF16), vmem((D, L), BF16), vmem((D, L), BF16),
+            vmem((L, D), BF16), vmem((L, D), BF16), vmem((D // 2, L), BF16), vmem((D // 2, L), BF16),
+            vmem((L, D // 2), BF16), vmem((L, D // 2), BF16), vmem((D // 2, L), BF16), vmem((D // 2, L), BF16),
             vmem((3, E, rows, H), BF16),
             vmem((3, S, rows, H), BF16),
-            vmem((3, D, H), BF16),
-            vmem((3, S, rows, H), BF16),
+            vmem((2, D, H), BF16),
+            vmem((2, D // 2, H), BF16),
+            vmem((3, S // 2, rows, H), BF16), vmem((3, S // 2, rows, H), BF16),
             vmem((3, R, S, rows, H), BF16),
             vmem((3, EL, rows, H), BF16),
             vmem((L, D), BF16),
@@ -327,10 +433,13 @@
             vmem((S * T, E * T), BF16),
             vmem((EL * T, R * S * T), BF16),
             vmem((L, H), F32), vmem((L, H), F32), vmem((L, H), F32),
-            vmem((L, H), BF16), vmem((L, H), BF16), vmem((L, H), BF16),
+            vmem((L, H), BF16), vmem((L, H), BF16),
+            vmem((3, L, H), BF16), vmem((3, L, H), BF16),
             dma((5,)), dma((4,)),
-            dma((3, S)), dma((3, S)), dma((3, Q, S)), dma((3, Q, S)),
-            dma((3, Q, chips)), dma((3, Q, chips)), dma((3, Q, chips)), dma((3, Q, chips)),
+            dma((2, S)), dma((2, S)), dma((2, S // 2)), dma((2, S // 2)),
+            dma((6,)), dma((6,)),
+            dma((3, S // 2)), dma((3, S // 2)), dma((3, Q, S // 2)), dma((3, Q, S // 2)),
+            dma((3, Q + 1, chips)), dma((3, Q + 1, chips)), dma((3, Q + 1, chips)), dma((3, Q + 1, chips)),
             dma((R,)), dma((R,)),
         ],
         compiler_params=pltpu.CompilerParams(
@@ -409,7 +518,7 @@
 
     def body(tokens, cotangent, coefficients, w_gate, w_up, w_down):
         args = (tokens, cotangent, coefficients, w_gate, w_up, w_down)
-        if w_gate.shape[1] % 128 == 0 and R % 2 == 0 and tokens.shape[1] % 128 == 0:
+        if w_gate.shape[1] % 128 == 0 and R % 2 == 0 and S % 2 == 0 and tokens.shape[1] % 128 == 0:
             return fused(S, R, *args)
         return local(*args)
 

time: 166 us -> 164 us (0.988); the launches traced: 163 us -> 163 us
  no operation moved by 1% of the time
where the time goes in v3:
time: 164 us; the launch traced here: 163 us
  Pallas kernels  162 us (99%)
    pallas_call x1, Pallas kernels, fused(): pl.pallas_call(functools.partial(kernel, S, R, Q), out_shape=(jax.ShapeDt...  159 us

profile of v3, /device:TPU:21, one launch (start us, length us, event | category | flops | bytes accessed | tf_op | source)
XLA Modules:
  0.0 162.7 jit_solution(7246008018441754255)
XLA Ops:
  0.6 158.9 %shard_map.93 = (bf16[1,256,1024]{2,1,0:T(8,128)(2,1)}, bf16[8,128,512]{2,1,0:T(8,128)(2,1)}, bf16[8,128,512]{2,1,0:T(8,128)(2,1)}, bf16[8,128,512]{2,1,0:T(8,128)(2,1)}) custom-call(bf16[1,8,32]{2,1,0:T(8,128)(2,1)} %coef_ref.1, bf16[1,256,1024]{2,1,0:T(8,128)(2,1)} %tok_hbm.1, bf16[1,256,1024]{2,1,0:T(8,128)(2,1)} %cot_hbm.1, ...), custom_call_target="tpu_custom_call" | custom-call | flops 5368709120 | bytes 17301504 | tf_op jit(solution)/shard_map/pallas_call | solution.py:416
  159.5 3.2 %shard_map.94 = (bf16[1,256,1024]{2,1,0:T(8,128)(2,1)}, bf16[8,128,512]{2,1,0:T(8,128)(2,1)}, bf16[8,128,512]{2,1,0:T(8,128)(2,1)}, bf16[8,128,512]{2,1,0:T(8,128)(2,1)}) custom-call(bf16[1,256,1024]{2,1,0:T(8,128)(2,1)} %get-tuple-element.8.refs_0_, bf16[8,128,512]{2,1,0:T(8,128)(2,1)} %get-tuple-element.9.refs_1_, ...), custom_call_target="tpu_custom_call" | custom-call | bytes 7340032 | tf_op jit(solution)/shard_map/pallas_call | solution.py:393

commit v4 on v3

--- a/solution.py
+++ b/solution.py
@@ -12,6 +12,9 @@
 BF16 = jnp.bfloat16
 T = 16
 GATE, UP, DOWN = 0, 1, 2
+PIECES = {GATE: 2, UP: 4, DOWN: 2}
+MOST = max(PIECES.values())
+HEAD = 32
 
 
 def one_hot(shape, rows_of, columns_of):
@@ -29,7 +32,7 @@
 
 
 def kernel(
-    S, R, Q, coef_ref, tok_hbm, cot_hbm, wg_hbm, wu_hbm, wd_hbm,
+    S, R, coef_ref, tok_hbm, cot_hbm, wg_hbm, wu_hbm, wd_hbm,
     ig_hbm, gg_hbm, gu_hbm, gd_hbm,
     x, g, xt, gt, xp, gp, xpt, gpt, w, msend, mfull, mdown, gown, ghelp, gall, outv, igv, cbuf, mix, fold,
     gate_s, up_s, dh_s, dhp_s, dhr, d_s, dr,
@@ -75,9 +78,15 @@
 
     loads = [pltpu.make_async_copy(tok_hbm.at[0], x, load_sem.at[0]),
              pltpu.make_async_copy(cot_hbm.at[0], g, load_sem.at[1])]
-    w_loads = [pltpu.make_async_copy(h, w.at[p], load_sem.at[2 + p])
-               for p, h in enumerate((wg_hbm, wu_hbm, wd_hbm))]
-    for c in w_loads + loads:
+    w_loads = {p: pltpu.make_async_copy(h, w.at[p], load_sem.at[1 + p])
+               for p, h in ((UP, wu_hbm), (DOWN, wd_hbm))}
+
+    def head(n):
+        return pl.ds(n * HEAD, HEAD)
+
+    heads = [pltpu.make_async_copy(wg_hbm.at[:, head(n), :], w.at[GATE, :, head(n), :], load_sem.at[4 + n])
+             for n in range(rows // HEAD)]
+    for c in heads:
         c.start()
 
     barrier = pltpu.get_barrier_semaphore()
@@ -126,27 +135,45 @@
     x_out = to_partner(0, x.at[:, span(other, HS)], xp)
     g_out = to_partner(1, g.at[:, span(other, HS)], gp)
     dh_out = to_partner(2, dhp_s, dhr)
-    d_out = [to_partner(3 + p, d_s.at[p], dr.at[p]) for p in (GATE, UP, DOWN)]
-
-    for p in (GATE, UP, DOWN):
-        w_loads[p].wait()
-
-        def merge(b, p=p):
-            at = pl.ds(pl.multiple_of(b * T, T), T)
-            block = dot(mix[...], w[p, :, at, :].reshape(E * T, H))
-            msend[p, :, at, :] = block.astype(BF16).reshape(S, T, H)
-
-        loop(0, rows // T, merge)
-        if p == GATE:
-            loop(1, S, lambda k: merged_copy(GATE, k, me).start())
-        if p == DOWN:
-            for k in range(1, HS):
-                for t in range(2):
-                    down_copy(t, k, place).start()
-            mdown[0, span(place), :] = msend[DOWN, me]
-            mdown[1, span(place), :] = msend[DOWN, partner]
-        else:
-            mfull[p, span(me), :] = msend[p, me]
+
+    def columns(p, c):
+        width = H // PIECES[p]
+        return pl.ds(c * width, width)
+
+    d_out = [[to_partner(3 + p * MOST + c, d_s.at[p, :, columns(p, c)], dr.at[p, :, columns(p, c)])
+              for c in range(PIECES[p])] for p in (GATE, UP, DOWN)]
+
+    def merge(p, b):
+        at = pl.ds(pl.multiple_of(b * T, T), T)
+        block = dot(mix[...], w[p, :, at, :].reshape(E * T, H))
+        msend[p, :, at, :] = block.astype(BF16).reshape(S, T, H)
+
+    for n, c in enumerate(heads):
+        c.wait()
+        loop(n * HEAD // T, (n + 1) * HEAD // T, lambda b: merge(GATE, b))
+
+        def send_head(k, n=n):
+            pltpu.make_async_remote_copy(
+                src_ref=msend.at[GATE, seg_at(k), head(n)],
+                dst_ref=mfull.at[GATE, pl.ds(pl.multiple_of(me * rows, rows) + n * HEAD, HEAD)],
+                send_sem=fsend.at[GATE, k], recv_sem=frecv.at[GATE, k],
+                device_id={"seg": seg_at(k)}, device_id_type=MESH).start()
+
+        loop(1, S, send_head)
+        if n == 0:
+            for c in list(w_loads.values()) + loads:
+                c.start()
+    mfull[GATE, span(me), :] = msend[GATE, me]
+    w_loads[UP].wait()
+    loop(0, rows // T, lambda b: merge(UP, b))
+    mfull[UP, span(me), :] = msend[UP, me]
+    w_loads[DOWN].wait()
+    loop(0, rows // T, lambda b: merge(DOWN, b))
+    for k in range(1, HS):
+        for t in range(2):
+            down_copy(t, k, place).start()
+    mdown[0, span(place), :] = msend[DOWN, me]
+    mdown[1, span(place), :] = msend[DOWN, partner]
 
     for c in loads:
         c.wait()
@@ -161,10 +188,7 @@
     keep = one_hot((EL * T, R * S * T), lambda i: i % T, lambda j: j % T)
     fold[...] = jnp.where(keep, wide, 0.0).astype(BF16)
 
-    part = rows // Q
-
-    def piece(c):
-        return pl.ds(c * part, part)
+    WHOLE = MOST
 
     def own_copy(p, k, owner):
         return pltpu.make_async_remote_copy(
@@ -174,14 +198,15 @@
 
     def help_copy(p, c, k, owner):
         return pltpu.make_async_remote_copy(
-            src_ref=ghelp.at[p, k, piece(c)], dst_ref=gall.at[p, rep, other + owner, piece(c)],
+            src_ref=ghelp.at[p, k, :, columns(p, c)],
+            dst_ref=gall.at[p, rep, other + owner, :, columns(p, c)],
             send_sem=hsend.at[p, c, k], recv_sem=hrecv.at[p, c, k],
             device_id={"seg": base + place_at(k)}, device_id_type=MESH)
 
     def unit(p, c, owner):
-        if c == Q:
+        if c == WHOLE:
             return gall.at[p, owner, pl.ds(base, HS)]
-        return gall.at[p, owner, pl.ds(other, HS), piece(c)]
+        return gall.at[p, owner, pl.ds(other, HS), :, columns(p, c)]
 
     def chip_copy(p, c, j, owner):
         block = unit(p, c, owner)
@@ -210,23 +235,23 @@
         loop(1, HS, step)
         gall[p, rep, me] = one(0)
 
-    def make_help(p):
+    def make_help(p, c):
+        d_out[p][c].wait_recv()
         transposed = gpt if p == DOWN else xpt
 
         def one(k):
-            return dot(transposed[span(place_at(k)), :], dr[p]).astype(BF16)
+            return dot(transposed[span(place_at(k)), :], dr[p, :, columns(p, c)]).astype(BF16)
 
         def step(k):
-            ghelp[p, k] = one(k)
+            ghelp[p, k, :, columns(p, c)] = one(k)
+            help_copy(p, c, k, place).start()
 
         loop(1, HS, step)
-        gall[p, rep, partner] = one(0)
-        for c in range(Q):
-            loop(1, HS, lambda k, c=c: help_copy(p, c, k, place).start())
+        gall[p, rep, partner, :, columns(p, c)] = one(0)
 
     def pass_on(p, c):
         def arrived(k):
-            if c == Q:
+            if c == WHOLE:
                 own_copy(p, k, place_from(k)).wait_recv()
             else:
                 help_copy(p, c, k, place_from(k)).wait_recv()
@@ -249,11 +274,12 @@
         collect(p, c)
 
         def folded(b):
-            at = pl.ds(pl.multiple_of(c * part + b * T, T), T)
-            block = dot(fold[...], gall[p, :, :, at, :].reshape(R * S * T, H))
-            outv[p, :, at, :] = block.astype(BF16).reshape(EL, T, H)
-
-        loop(0, part // T, folded)
+            at = pl.ds(pl.multiple_of(b * T, T), T)
+            width = H // PIECES[p]
+            block = dot(fold[...], gall[p, :, :, at, columns(p, c)].reshape(R * S * T, width))
+            outv[p, :, at, columns(p, c)] = block.astype(BF16).reshape(EL, T, width)
+
+        loop(0, rows // T, folded)
 
     outs = (gg_hbm, gu_hbm, gd_hbm)
     out_copies = [pltpu.make_async_copy(outv.at[p], outs[p], out_sem.at[p]) for p in (GATE, UP, DOWN)]
@@ -285,17 +311,20 @@
         d_s[DOWN, at, :] = (gate * jax.nn.sigmoid(gate) * up_s[at, :]).astype(BF16)
 
     loop(0, L // CH, hidden)
-    d_out[DOWN].start()
+    for c in d_out[DOWN]:
+        c.start()
     make_own(DOWN)
     g_out.wait_recv()
     dhp_s[...] = dot(gp[...], mdown[1]).astype(BF16)
     dh_out.start()
     gpt[...] = gp[...].T
     x_out.start()
-    pass_on(DOWN, Q)
-    d_out[DOWN].wait_recv()
-    make_help(DOWN)
-
+    pass_on(DOWN, WHOLE)
+    for c in range(PIECES[DOWN]):
+        make_help(DOWN, c)
+    hand_over(DOWN, WHOLE)
+    for c in range(PIECES[DOWN]):
+        pass_on(DOWN, c)
     dh_out.wait_recv()
 
     def backward(i):
@@ -307,17 +336,12 @@
         d_s[UP, at, :] = (dh * (gate * sigma)).astype(BF16)
 
     loop(0, L // CH, backward)
-    d_out[GATE].start()
+    for c in d_out[GATE] + d_out[UP]:
+        c.start()
     make_own(GATE)
     make_own(UP)
-    for c in range(Q):
-        pass_on(DOWN, c)
-    x_out.wait_recv()
-    xpt[...] = xp[...].T
-    d_out[GATE].wait_send()
-    d_out[UP].start()
-    pass_on(GATE, Q)
-    hand_over(DOWN, Q)
+    pass_on(GATE, WHOLE)
+    pass_on(UP, WHOLE)
 
     def input_grad(i):
         at = span(i)
@@ -326,27 +350,28 @@
 
     loop(0, S, input_grad)
     ig_copy.start()
-    pass_on(UP, Q)
-    d_out[GATE].wait_recv()
-    make_help(GATE)
-    collect(DOWN, Q)
-    for c in range(Q):
+    x_out.wait_recv()
+    xpt[...] = xp[...].T
+    for c in range(PIECES[DOWN]):
         hand_over(DOWN, c)
-    for c in range(Q):
-        pass_on(GATE, c)
-    for c in range(Q):
+    collect(DOWN, WHOLE)
+    for c in range(PIECES[DOWN]):
         fold_piece(DOWN, c)
     out_copies[DOWN].start()
-    d_out[UP].wait_recv()
-    make_help(UP)
-    hand_over(GATE, Q)
-    hand_over(UP, Q)
-    for c in range(Q):
+    for c in range(PIECES[GATE]):
+        make_help(GATE, c)
+    hand_over(GATE, WHOLE)
+    for c in range(PIECES[GATE]):
+        pass_on(GATE, c)
+    for c in range(PIECES[UP]):
+        make_help(UP, c)
+    hand_over(UP, WHOLE)
+    for c in range(PIECES[UP]):
         pass_on(UP, c)
     for p in (GATE, UP):
-        collect(p, Q)
-        for c in range(Q + 1):
-            if c < Q:
+        collect(p, WHOLE)
+        for c in range(PIECES[p] + 1):
+            if c < PIECES[p]:
                 hand_over(p, c)
             if c > 0:
                 fold_piece(p, c - 1)
@@ -355,16 +380,16 @@
     for k in range(1, R):
         coef_copy(k, rep).wait_send()
     loop(1, S, lambda k: merged_copy(UP, k, me).wait_send())
-    for c in (x_out, g_out, dh_out, d_out[UP], d_out[DOWN]):
+    for c in [x_out, g_out, dh_out] + d_out[GATE] + d_out[UP] + d_out[DOWN]:
         c.wait_send()
     for k in range(1, HS):
         for t in range(2):
             down_copy(t, k, place).wait_send()
     for p in (GATE, UP, DOWN):
         loop(1, HS, lambda k, p=p: own_copy(p, k, place).wait_send())
-        for c in range(Q):
+        for c in range(PIECES[p]):
             loop(1, HS, lambda k, p=p, c=c: help_copy(p, c, k, place).wait_send())
-        for c in range(Q + 1):
+        for c in [*range(PIECES[p]), WHOLE]:
             for j in range(1, chips):
                 chip_copy(p, c, j, rep).wait_send()
             for j in range(chips):
@@ -412,9 +437,9 @@
     vmem = pltpu.VMEM
     grad = jax.ShapeDtypeStruct((EL, rows, H), BF16)
     flops = 16 * L * D * H + 2 * 3 * T * rows * H * E * S + 2 * 3 * T * rows * H * EL * R * S
-    Q = 4
+    Q = MOST
     made = pl.pallas_call(
-        functools.partial(kernel, S, R, Q),
+        functools.partial(kernel, S, R),
         out_shape=(jax.ShapeDtypeStruct((1, L, D), BF16), grad, grad, grad),
         in_specs=[pl.BlockSpec(memory_space=vmem)] + [any_spec] * 5,
         out_specs=(any_spec,) * 4,
@@ -435,9 +460,9 @@
             vmem((L, H), F32), vmem((L, H), F32), vmem((L, H), F32),
             vmem((L, H), BF16), vmem((L, H), BF16),
             vmem((3, L, H), BF16), vmem((3, L, H), BF16),
-            dma((5,)), dma((4,)),
+            dma((4 + rows // HEAD,)), dma((4,)),
             dma((2, S)), dma((2, S)), dma((2, S // 2)), dma((2, S // 2)),
-            dma((6,)), dma((6,)),
+            dma((3 + 3 * Q,)), dma((3 + 3 * Q,)),
             dma((3, S // 2)), dma((3, S // 2)), dma((3, Q, S // 2)), dma((3, Q, S // 2)),
             dma((3, Q + 1, chips)), dma((3, Q + 1, chips)), dma((3, Q + 1, chips)), dma((3, Q + 1, chips)),
             dma((R,)), dma((R,)),
@@ -518,7 +543,7 @@
 
     def body(tokens, cotangent, coefficients, w_gate, w_up, w_down):
         args = (tokens, cotangent, coefficients, w_gate, w_up, w_down)
-        if w_gate.shape[1] % 128 == 0 and R % 2 == 0 and S % 2 == 0 and tokens.shape[1] % 128 == 0:
+        if w_gate.shape[1] % 128 == 0 and w_gate.shape[2] % (128 * MOST) == 0 and R % 2 == 0 and S % 2 == 0 and tokens.shape[1] % 128 == 0:
             return fused(S, R, *args)
         return local(*args)
 

time: 164 us -> 167 us (1.018)
  Pallas kernels: 162 us -> 164 us
    pallas_call x1, Pallas kernels: 159 us -> 161 us  [fused(): pl.pallas_call(functools.partial(kernel, S, R), out_shape=(jax.ShapeDtype...]
where the time goes in v4:
time: 167 us; the launch traced here: 165 us
  Pallas kernels  164 us (98%)
    pallas_call x1, Pallas kernels, fused(): pl.pallas_call(functools.partial(kernel, S, R), out_shape=(jax.ShapeDtype...  161 us

profile of v4, /device:TPU:21, one launch (start us, length us, event | category | flops | bytes accessed | tf_op | source)
XLA Modules:
  0.0 165.1 jit_solution(7798931222075295110)
XLA Ops:
  0.6 161.3 %shard_map.93 = (bf16[1,256,1024]{2,1,0:T(8,128)(2,1)}, bf16[8,128,512]{2,1,0:T(8,128)(2,1)}, bf16[8,128,512]{2,1,0:T(8,128)(2,1)}, bf16[8,128,512]{2,1,0:T(8,128)(2,1)}) custom-call(bf16[1,8,32]{2,1,0:T(8,128)(2,1)} %coef_ref.1, bf16[1,256,1024]{2,1,0:T(8,128)(2,1)} %tok_hbm.1, bf16[1,256,1024]{2,1,0:T(8,128)(2,1)} %cot_hbm.1, ...), custom_call_target="tpu_custom_call" | custom-call | flops 5368709120 | bytes 17301504 | tf_op jit(solution)/shard_map/pallas_call | solution.py:441
  161.9 3.2 %shard_map.94 = (bf16[1,256,1024]{2,1,0:T(8,128)(2,1)}, bf16[8,128,512]{2,1,0:T(8,128)(2,1)}, bf16[8,128,512]{2,1,0:T(8,128)(2,1)}, bf16[8,128,512]{2,1,0:T(8,128)(2,1)}) custom-call(bf16[1,256,1024]{2,1,0:T(8,128)(2,1)} %get-tuple-element.8.refs_0_, bf16[8,128,512]{2,1,0:T(8,128)(2,1)} %get-tuple-element.9.refs_1_, ...), custom_call_target="tpu_custom_call" | custom-call | bytes 7340032 | tf_op jit(solution)/shard_map/pallas_call | solution.py:418

commit v5 on v4

--- a/solution.py
+++ b/solution.py
@@ -12,8 +12,7 @@
 BF16 = jnp.bfloat16
 T = 16
 GATE, UP, DOWN = 0, 1, 2
-PIECES = {GATE: 2, UP: 4, DOWN: 2}
-MOST = max(PIECES.values())
+Q = 4
 HEAD = 32
 
 
@@ -135,13 +134,7 @@
     x_out = to_partner(0, x.at[:, span(other, HS)], xp)
     g_out = to_partner(1, g.at[:, span(other, HS)], gp)
     dh_out = to_partner(2, dhp_s, dhr)
-
-    def columns(p, c):
-        width = H // PIECES[p]
-        return pl.ds(c * width, width)
-
-    d_out = [[to_partner(3 + p * MOST + c, d_s.at[p, :, columns(p, c)], dr.at[p, :, columns(p, c)])
-              for c in range(PIECES[p])] for p in (GATE, UP, DOWN)]
+    d_out = [to_partner(3 + p, d_s.at[p], dr.at[p]) for p in (GATE, UP, DOWN)]
 
     def merge(p, b):
         at = pl.ds(pl.multiple_of(b * T, T), T)
@@ -188,7 +181,11 @@
     keep = one_hot((EL * T, R * S * T), lambda i: i % T, lambda j: j % T)
     fold[...] = jnp.where(keep, wide, 0.0).astype(BF16)
 
-    WHOLE = MOST
+    WHOLE = Q
+    part = rows // Q
+
+    def piece(c):
+        return pl.ds(c * part, part)
 
     def own_copy(p, k, owner):
         return pltpu.make_async_remote_copy(
@@ -198,15 +195,14 @@
 
     def help_copy(p, c, k, owner):
         return pltpu.make_async_remote_copy(
-            src_ref=ghelp.at[p, k, :, columns(p, c)],
-            dst_ref=gall.at[p, rep, other + owner, :, columns(p, c)],
+            src_ref=ghelp.at[p, k, piece(c)], dst_ref=gall.at[p, rep, other + owner, piece(c)],
             send_sem=hsend.at[p, c, k], recv_sem=hrecv.at[p, c, k],
             device_id={"seg": base + place_at(k)}, device_id_type=MESH)
 
     def unit(p, c, owner):
         if c == WHOLE:
             return gall.at[p, owner, pl.ds(base, HS)]
-        return gall.at[p, owner, pl.ds(other, HS), :, columns(p, c)]
+        return gall.at[p, owner, pl.ds(other, HS), piece(c)]
 
     def chip_copy(p, c, j, owner):
         block = unit(p, c, owner)
@@ -235,19 +231,21 @@
         loop(1, HS, step)
         gall[p, rep, me] = one(0)
 
-    def make_help(p, c):
-        d_out[p][c].wait_recv()
+    def make_help(p):
+        d_out[p].wait_recv()
         transposed = gpt if p == DOWN else xpt
 
         def one(k):
-            return dot(transposed[span(place_at(k)), :], dr[p, :, columns(p, c)]).astype(BF16)
+            return dot(transposed[span(place_at(k)), :], dr[p]).astype(BF16)
 
         def step(k):
-            ghelp[p, k, :, columns(p, c)] = one(k)
-            help_copy(p, c, k, place).start()
+            ghelp[p, k] = one(k)
+            help_copy(p, 0, k, place).start()
 
         loop(1, HS, step)
-        gall[p, rep, partner, :, columns(p, c)] = one(0)
+        for c in range(1, Q):
+            loop(1, HS, lambda k, c=c: help_copy(p, c, k, place).start())
+        gall[p, rep, partner] = one(0)
 
     def pass_on(p, c):
         def arrived(k):
@@ -274,12 +272,11 @@
         collect(p, c)
 
         def folded(b):
-            at = pl.ds(pl.multiple_of(b * T, T), T)
-            width = H // PIECES[p]
-            block = dot(fold[...], gall[p, :, :, at, columns(p, c)].reshape(R * S * T, width))
-            outv[p, :, at, columns(p, c)] = block.astype(BF16).reshape(EL, T, width)
-
-        loop(0, rows // T, folded)
+            at = pl.ds(pl.multiple_of(c * part + b * T, T), T)
+            block = dot(fold[...], gall[p, :, :, at, :].reshape(R * S * T, H))
+            outv[p, :, at, :] = block.astype(BF16).reshape(EL, T, H)
+
+        loop(0, part // T, folded)
 
     outs = (gg_hbm, gu_hbm, gd_hbm)
     out_copies = [pltpu.make_async_copy(outv.at[p], outs[p], out_sem.at[p]) for p in (GATE, UP, DOWN)]
@@ -290,14 +287,14 @@
         merged_copy(UP, k, me).start()
 
     loop(1, S, send_up)
-    g_out.start()
     loop(1, S, lambda k: merged_copy(GATE, k, seg_from(k)).wait_recv())
     gate_s[...] = dot(x[...], mfull[GATE])
     for k in range(1, HS):
         for t in range(2):
             down_copy(t, k, place_from(k)).wait_recv()
     dh_s[...] = dot(g[:, span(base, HS)], mdown[0])
-
+    loop(1, S, lambda k: merged_copy(UP, k, me).wait_send())
+    g_out.start()
     loop(1, S, lambda k: merged_copy(UP, k, seg_from(k)).wait_recv())
     up_s[...] = dot(x[...], mfull[UP])
     CH = 32
@@ -311,20 +308,15 @@
         d_s[DOWN, at, :] = (gate * jax.nn.sigmoid(gate) * up_s[at, :]).astype(BF16)
 
     loop(0, L // CH, hidden)
-    for c in d_out[DOWN]:
-        c.start()
+    d_out[DOWN].start()
     make_own(DOWN)
     g_out.wait_recv()
     dhp_s[...] = dot(gp[...], mdown[1]).astype(BF16)
     dh_out.start()
     gpt[...] = gp[...].T
+    pass_on(DOWN, WHOLE)
+    make_help(DOWN)
     x_out.start()
-    pass_on(DOWN, WHOLE)
-    for c in range(PIECES[DOWN]):
-        make_help(DOWN, c)
-    hand_over(DOWN, WHOLE)
-    for c in range(PIECES[DOWN]):
-        pass_on(DOWN, c)
     dh_out.wait_recv()
 
     def backward(i):
@@ -336,12 +328,14 @@
         d_s[UP, at, :] = (dh * (gate * sigma)).astype(BF16)
 
     loop(0, L // CH, backward)
-    for c in d_out[GATE] + d_out[UP]:
-        c.start()
+    d_out[GATE].start()
     make_own(GATE)
     make_own(UP)
+    for c in range(Q):
+        pass_on(DOWN, c)
     pass_on(GATE, WHOLE)
     pass_on(UP, WHOLE)
+    hand_over(DOWN, WHOLE)
 
     def input_grad(i):
         at = span(i)
@@ -352,26 +346,26 @@
     ig_copy.start()
     x_out.wait_recv()
     xpt[...] = xp[...].T
-    for c in range(PIECES[DOWN]):
+    d_out[GATE].wait_send()
+    d_out[UP].start()
+    for c in range(Q):
         hand_over(DOWN, c)
     collect(DOWN, WHOLE)
-    for c in range(PIECES[DOWN]):
+    make_help(GATE)
+    for c in range(Q):
         fold_piece(DOWN, c)
     out_copies[DOWN].start()
-    for c in range(PIECES[GATE]):
-        make_help(GATE, c)
     hand_over(GATE, WHOLE)
-    for c in range(PIECES[GATE]):
+    for c in range(Q):
         pass_on(GATE, c)
-    for c in range(PIECES[UP]):
-        make_help(UP, c)
+    make_help(UP)
     hand_over(UP, WHOLE)
-    for c in range(PIECES[UP]):
+    for c in range(Q):
         pass_on(UP, c)
     for p in (GATE, UP):
         collect(p, WHOLE)
-        for c in range(PIECES[p] + 1):
-            if c < PIECES[p]:
+        for c in range(Q + 1):
+            if c < Q:
                 hand_over(p, c)
             if c > 0:
                 fold_piece(p, c - 1)
@@ -379,17 +373,16 @@
 
     for k in range(1, R):
         coef_copy(k, rep).wait_send()
-    loop(1, S, lambda k: merged_copy(UP, k, me).wait_send())
-    for c in [x_out, g_out, dh_out] + d_out[GATE] + d_out[UP] + d_out[DOWN]:
+    for c in (x_out, g_out, dh_out, d_out[UP], d_out[DOWN]):
         c.wait_send()
     for k in range(1, HS):
         for t in range(2):
             down_copy(t, k, place).wait_send()
     for p in (GATE, UP, DOWN):
         loop(1, HS, lambda k, p=p: own_copy(p, k, place).wait_send())
-        for c in range(PIECES[p]):
+        for c in range(Q):
             loop(1, HS, lambda k, p=p, c=c: help_copy(p, c, k, place).wait_send())
-        for c in [*range(PIECES[p]), WHOLE]:
+        for c in [*range(Q), WHOLE]:
             for j in range(1, chips):
                 chip_copy(p, c, j, rep).wait_send()
             for j in range(chips):
@@ -437,7 +430,6 @@
     vmem = pltpu.VMEM
     grad = jax.ShapeDtypeStruct((EL, rows, H), BF16)
     flops = 16 * L * D * H + 2 * 3 * T * rows * H * E * S + 2 * 3 * T * rows * H * EL * R * S
-    Q = MOST
     made = pl.pallas_call(
         functools.partial(kernel, S, R),
         out_shape=(jax.ShapeDtypeStruct((1, L, D), BF16), grad, grad, grad),
@@ -462,7 +454,7 @@
             vmem((3, L, H), BF16), vmem((3, L, H), BF16),
             dma((4 + rows // HEAD,)), dma((4,)),
             dma((2, S)), dma((2, S)), dma((2, S // 2)), dma((2, S // 2)),
-            dma((3 + 3 * Q,)), dma((3 + 3 * Q,)),
+            dma((6,)), dma((6,)),
             dma((3, S // 2)), dma((3, S // 2)), dma((3, Q, S // 2)), dma((3, Q, S // 2)),
             dma((3, Q + 1, chips)), dma((3, Q + 1, chips)), dma((3, Q + 1, chips)), dma((3, Q + 1, chips)),
             dma((R,)), dma((R,)),
@@ -543,7 +535,7 @@
 
     def body(tokens, cotangent, coefficients, w_gate, w_up, w_down):
         args = (tokens, cotangent, coefficients, w_gate, w_up, w_down)
-        if w_gate.shape[1] % 128 == 0 and w_gate.shape[2] % (128 * MOST) == 0 and R % 2 == 0 and S % 2 == 0 and tokens.shape[1] % 128 == 0:
+        if w_gate.shape[1] % 128 == 0 and R % 2 == 0 and S % 2 == 0 and tokens.shape[1] % 128 == 0:
             return fused(S, R, *args)
         return local(*args)
 

time: 167 us -> 165 us (0.988)
  no operation moved by 1% of the time
where the time goes in v5:
time: 165 us
  Pallas kernels  164 us (99%)
    pallas_call x1, Pallas kernels, fused(): pl.pallas_call(functools.partial(kernel, S, R), out_shape=(jax.ShapeDtype...  161 us

profile of v5, /device:TPU:21, one launch (start us, length us, event | category | flops | bytes accessed | tf_op | source)
XLA Modules:
  0.0 164.6 jit_solution(6171953593864571692)
XLA Ops:
  0.6 160.8 %shard_map.93 = (bf16[1,256,1024]{2,1,0:T(8,128)(2,1)}, bf16[8,128,512]{2,1,0:T(8,128)(2,1)}, bf16[8,128,512]{2,1,0:T(8,128)(2,1)}, bf16[8,128,512]{2,1,0:T(8,128)(2,1)}) custom-call(bf16[1,8,32]{2,1,0:T(8,128)(2,1)} %coef_ref.1, bf16[1,256,1024]{2,1,0:T(8,128)(2,1)} %tok_hbm.1, bf16[1,256,1024]{2,1,0:T(8,128)(2,1)} %cot_hbm.1, ...), custom_call_target="tpu_custom_call" | custom-call | flops 5368709120 | bytes 17301504 | tf_op jit(solution)/shard_map/pallas_call | solution.py:433
  161.5 3.2 %shard_map.94 = (bf16[1,256,1024]{2,1,0:T(8,128)(2,1)}, bf16[8,128,512]{2,1,0:T(8,128)(2,1)}, bf16[8,128,512]{2,1,0:T(8,128)(2,1)}, bf16[8,128,512]{2,1,0:T(8,128)(2,1)}) custom-call(bf16[1,256,1024]{2,1,0:T(8,128)(2,1)} %get-tuple-element.8.refs_0_, bf16[8,128,512]{2,1,0:T(8,128)(2,1)} %get-tuple-element.9.refs_1_, ...), custom_call_target="tpu_custom_call" | custom-call | bytes 7340032 | tf_op jit(solution)/shard_map/pallas_call | solution.py:411

commit v6 on v5

--- a/solution.py
+++ b/solution.py
@@ -11,8 +11,8 @@
 F32 = jnp.float32
 BF16 = jnp.bfloat16
 T = 16
-GATE, UP, DOWN = 0, 1, 2
-Q = 4
+GATE, UP, DOWN = 0, 2, 4
+Q = 2
 HEAD = 32
 
 
@@ -41,6 +41,7 @@
     me = lax.axis_index("seg")
     rep = lax.axis_index("rep")
     E, rows, H = w.shape[1:]
+    HH = H // 2
     EL = outv.shape[1]
     L = x.shape[0]
     chips = R // 2
@@ -77,7 +78,7 @@
 
     loads = [pltpu.make_async_copy(tok_hbm.at[0], x, load_sem.at[0]),
              pltpu.make_async_copy(cot_hbm.at[0], g, load_sem.at[1])]
-    w_loads = {p: pltpu.make_async_copy(h, w.at[p], load_sem.at[1 + p])
+    w_loads = {p: pltpu.make_async_copy(h, w.at[p // 2], load_sem.at[1 + p // 2])
                for p, h in ((UP, wu_hbm), (DOWN, wd_hbm))}
 
     def head(n):
@@ -119,11 +120,11 @@
             send_sem=fsend.at[p, k], recv_sem=frecv.at[p, k],
             device_id={"seg": seg_at(k)}, device_id_type=MESH)
 
-    def down_copy(t, k, owner):
+    def down_copy(h, t, k, owner):
         to = place_at(k)
         return pltpu.make_async_remote_copy(
-            src_ref=msend.at[DOWN, (base if t == 0 else other) + to], dst_ref=mdown.at[t, span(owner)],
-            send_sem=dsend.at[t, k], recv_sem=drecv.at[t, k],
+            src_ref=msend.at[DOWN + h, (base if t == 0 else other) + to], dst_ref=mdown.at[h, t, span(owner)],
+            send_sem=dsend.at[h, t, k], recv_sem=drecv.at[h, t, k],
             device_id={"seg": base + to}, device_id_type=MESH)
 
     def to_partner(n, source, target):
@@ -133,13 +134,14 @@
 
     x_out = to_partner(0, x.at[:, span(other, HS)], xp)
     g_out = to_partner(1, g.at[:, span(other, HS)], gp)
-    dh_out = to_partner(2, dhp_s, dhr)
-    d_out = [to_partner(3 + p, d_s.at[p], dr.at[p]) for p in (GATE, UP, DOWN)]
+    dh_out = [to_partner(2 + h, dhp_s.at[h], dhr.at[h]) for h in range(2)]
+    d_out = [to_partner(4 + p, d_s.at[p], dr.at[p]) for p in range(6)]
 
     def merge(p, b):
         at = pl.ds(pl.multiple_of(b * T, T), T)
-        block = dot(mix[...], w[p, :, at, :].reshape(E * T, H))
-        msend[p, :, at, :] = block.astype(BF16).reshape(S, T, H)
+        block = dot(mix[...], w[p // 2, :, at, :].reshape(E * T, H)).astype(BF16)
+        for h in range(2):
+            msend[p + h, :, at, :] = block[:, h * HH:(h + 1) * HH].reshape(S, T, HH)
 
     for n, c in enumerate(heads):
         c.wait()
@@ -156,17 +158,22 @@
         if n == 0:
             for c in list(w_loads.values()) + loads:
                 c.start()
-    mfull[GATE, span(me), :] = msend[GATE, me]
+
+    def send_down(h):
+        for k in range(1, HS):
+            for t in range(2):
+                down_copy(h, t, k, place).start()
+
     w_loads[UP].wait()
     loop(0, rows // T, lambda b: merge(UP, b))
-    mfull[UP, span(me), :] = msend[UP, me]
+    for v in (GATE, GATE + 1, UP, UP + 1):
+        mfull[v, span(me), :] = msend[v, me]
     w_loads[DOWN].wait()
     loop(0, rows // T, lambda b: merge(DOWN, b))
-    for k in range(1, HS):
-        for t in range(2):
-            down_copy(t, k, place).start()
-    mdown[0, span(place), :] = msend[DOWN, me]
-    mdown[1, span(place), :] = msend[DOWN, partner]
+    send_down(0)
+    for h in range(2):
+        mdown[h, 0, span(place), :] = msend[DOWN + h, me]
+        mdown[h, 1, span(place), :] = msend[DOWN + h, partner]
 
     for c in loads:
         c.wait()
@@ -219,7 +226,7 @@
             device_id={"rep": sibling}, device_id_type=MESH)
 
     def make_own(p):
-        transposed = gt if p == DOWN else xt
+        transposed = gt if p >= DOWN else xt
 
         def one(k):
             return dot(transposed[span(place_at(k)), :], d_s[p]).astype(BF16)
@@ -233,7 +240,7 @@
 
     def make_help(p):
         d_out[p].wait_recv()
-        transposed = gpt if p == DOWN else xpt
+        transposed = gpt if p >= DOWN else xpt
 
         def one(k):
             return dot(transposed[span(place_at(k)), :], dr[p]).astype(BF16)
@@ -273,112 +280,156 @@
 
         def folded(b):
             at = pl.ds(pl.multiple_of(c * part + b * T, T), T)
-            block = dot(fold[...], gall[p, :, :, at, :].reshape(R * S * T, H))
-            outv[p, :, at, :] = block.astype(BF16).reshape(EL, T, H)
+            block = dot(fold[...], gall[p, :, :, at, :].reshape(R * S * T, HH))
+            lanes = pl.ds(p % 2 * HH, HH)
+            outv[p // 2, :, at, lanes] = block.astype(BF16).reshape(EL, T, HH)
 
         loop(0, part // T, folded)
 
     outs = (gg_hbm, gu_hbm, gd_hbm)
-    out_copies = [pltpu.make_async_copy(outv.at[p], outs[p], out_sem.at[p]) for p in (GATE, UP, DOWN)]
+    out_copies = [pltpu.make_async_copy(outv.at[n], outs[n], out_sem.at[n]) for n in range(3)]
     ig_copy = pltpu.make_async_copy(igv, ig_hbm.at[0], out_sem.at[3])
 
-    def send_up(k):
-        merged_copy(GATE, k, me).wait_send()
-        merged_copy(UP, k, me).start()
-
-    loop(1, S, send_up)
-    loop(1, S, lambda k: merged_copy(GATE, k, seg_from(k)).wait_recv())
-    gate_s[...] = dot(x[...], mfull[GATE])
-    for k in range(1, HS):
-        for t in range(2):
-            down_copy(t, k, place_from(k)).wait_recv()
-    dh_s[...] = dot(g[:, span(base, HS)], mdown[0])
-    loop(1, S, lambda k: merged_copy(UP, k, me).wait_send())
-    g_out.start()
-    loop(1, S, lambda k: merged_copy(UP, k, seg_from(k)).wait_recv())
-    up_s[...] = dot(x[...], mfull[UP])
+    def send_after(p, before):
+        def step(k):
+            merged_copy(before, k, me).wait_send()
+            merged_copy(p, k, me).start()
+
+        loop(1, S, step)
+
+    def arrive(p):
+        loop(1, S, lambda k: merged_copy(p, k, seg_from(k)).wait_recv())
+
+    def project_gate(h):
+        arrive(GATE + h)
+        gate_s[h] = dot(x[...], mfull[GATE + h])
+
+    def project_down(h):
+        for k in range(1, HS):
+            for t in range(2):
+                down_copy(h, t, k, place_from(k)).wait_recv()
+        dh_s[h] = dot(g[:, span(base, HS)], mdown[h, 0])
+
     CH = 32
 
     def chunk(i):
         return pl.ds(pl.multiple_of(i * CH, CH), CH)
 
-    def hidden(i):
-        at = chunk(i)
-        gate = gate_s[at, :]
-        d_s[DOWN, at, :] = (gate * jax.nn.sigmoid(gate) * up_s[at, :]).astype(BF16)
-
-    loop(0, L // CH, hidden)
-    d_out[DOWN].start()
-    make_own(DOWN)
-    g_out.wait_recv()
-    dhp_s[...] = dot(gp[...], mdown[1]).astype(BF16)
-    dh_out.start()
-    gpt[...] = gp[...].T
-    pass_on(DOWN, WHOLE)
-    make_help(DOWN)
-    x_out.start()
-    dh_out.wait_recv()
-
-    def backward(i):
-        at = chunk(i)
-        gate = gate_s[at, :]
-        dh = dh_s[at, :] + dhr[at, :].astype(F32)
-        sigma = jax.nn.sigmoid(gate)
-        d_s[GATE, at, :] = (dh * up_s[at, :] * sigma * (1.0 + gate * (1.0 - sigma))).astype(BF16)
-        d_s[UP, at, :] = (dh * (gate * sigma)).astype(BF16)
-
-    loop(0, L // CH, backward)
-    d_out[GATE].start()
-    make_own(GATE)
-    make_own(UP)
-    for c in range(Q):
-        pass_on(DOWN, c)
-    pass_on(GATE, WHOLE)
-    pass_on(UP, WHOLE)
-    hand_over(DOWN, WHOLE)
-
-    def input_grad(i):
-        at = span(i)
-        total = dot_t(d_s[GATE], mfull[GATE, at, :]) + dot_t(d_s[UP], mfull[UP, at, :])
-        igv[:, at] = total.astype(BF16)
-
-    loop(0, S, input_grad)
-    ig_copy.start()
-    x_out.wait_recv()
-    xpt[...] = xp[...].T
-    d_out[GATE].wait_send()
-    d_out[UP].start()
-    for c in range(Q):
-        hand_over(DOWN, c)
-    collect(DOWN, WHOLE)
-    make_help(GATE)
-    for c in range(Q):
-        fold_piece(DOWN, c)
-    out_copies[DOWN].start()
-    hand_over(GATE, WHOLE)
-    for c in range(Q):
-        pass_on(GATE, c)
-    make_help(UP)
-    hand_over(UP, WHOLE)
-    for c in range(Q):
-        pass_on(UP, c)
-    for p in (GATE, UP):
+    def make_hidden(h):
+        arrive(UP + h)
+        up_s[h] = dot(x[...], mfull[UP + h])
+
+        def hidden(i):
+            at = chunk(i)
+            gate = gate_s[h, at, :]
+            d_s[DOWN + h, at, :] = (gate * jax.nn.sigmoid(gate) * up_s[h, at, :]).astype(BF16)
+
+        loop(0, L // CH, hidden)
+        d_out[DOWN + h].start()
+        make_own(DOWN + h)
+
+    def help_down(h):
+        dhp_s[h] = dot(gp[...], mdown[h, 1]).astype(BF16)
+        dh_out[h].start()
+
+    def make_d(h):
+        dh_out[h].wait_recv()
+
+        def backward(i):
+            at = chunk(i)
+            gate = gate_s[h, at, :]
+            dh = dh_s[h, at, :] + dhr[h, at, :].astype(F32)
+            sigma = jax.nn.sigmoid(gate)
+            d_s[GATE + h, at, :] = (dh * up_s[h, at, :] * sigma * (1.0 + gate * (1.0 - sigma))).astype(BF16)
+            d_s[UP + h, at, :] = (dh * (gate * sigma)).astype(BF16)
+
+        loop(0, L // CH, backward)
+        d_out[GATE + h].start()
+        d_out[UP + h].start()
+        make_own(GATE + h)
+        make_own(UP + h)
+
+    def pass_pieces(p):
+        for c in range(Q):
+            pass_on(p, c)
+
+    def finish(p):
         collect(p, WHOLE)
         for c in range(Q + 1):
             if c < Q:
                 hand_over(p, c)
             if c > 0:
                 fold_piece(p, c - 1)
-        out_copies[p].start()
+
+    send_after(UP, GATE)
+    project_gate(0)
+    g_out.start()
+    project_down(0)
+    send_after(GATE + 1, UP)
+    make_hidden(0)
+    send_down(1)
+    g_out.wait_recv()
+    help_down(0)
+    gpt[...] = gp[...].T
+    pass_on(DOWN, WHOLE)
+    x_out.start()
+    make_help(DOWN)
+    send_after(UP + 1, GATE + 1)
+    make_d(0)
+    pass_pieces(DOWN)
+    pass_on(GATE, WHOLE)
+    pass_on(UP, WHOLE)
+    project_gate(1)
+    project_down(1)
+    help_down(1)
+    hand_over(DOWN, WHOLE)
+    make_hidden(1)
+    x_out.wait_recv()
+    xpt[...] = xp[...].T
+    make_help(GATE)
+    make_help(UP)
+    pass_on(DOWN + 1, WHOLE)
+    pass_pieces(GATE)
+    pass_pieces(UP)
+    make_help(DOWN + 1)
+    make_d(1)
+    pass_pieces(DOWN + 1)
+    pass_on(GATE + 1, WHOLE)
+    pass_on(UP + 1, WHOLE)
+
+    def input_grad(i):
+        at = span(i)
+        total = sum(dot_t(d_s[v], mfull[v, at, :]) for v in (GATE, GATE + 1, UP, UP + 1))
+        igv[:, at] = total.astype(BF16)
+
+    loop(0, S, input_grad)
+    ig_copy.start()
+    finish(DOWN)
+    hand_over(GATE, WHOLE)
+    hand_over(UP, WHOLE)
+    make_help(GATE + 1)
+    make_help(UP + 1)
+    pass_pieces(GATE + 1)
+    finish(GATE)
+    pass_pieces(UP + 1)
+    finish(UP)
+    hand_over(DOWN + 1, WHOLE)
+    hand_over(GATE + 1, WHOLE)
+    hand_over(UP + 1, WHOLE)
+    for p, n in ((DOWN, 2), (GATE, 0), (UP, 1)):
+        finish(p + 1)
+        out_copies[n].start()
 
     for k in range(1, R):
         coef_copy(k, rep).wait_send()
-    for c in (x_out, g_out, dh_out, d_out[UP], d_out[DOWN]):
+    loop(1, S, lambda k: merged_copy(UP + 1, k, me).wait_send())
+    for c in [x_out, g_out] + dh_out + d_out:
         c.wait_send()
     for k in range(1, HS):
-        for t in range(2):
-            down_copy(t, k, place).wait_send()
-    for p in (GATE, UP, DOWN):
+        for h in range(2):
+            for t in range(2):
+                down_copy(h, t, k, place).wait_send()
+    for p in range(6):
         loop(1, HS, lambda k, p=p: own_copy(p, k, place).wait_send())
         for c in range(Q):
             loop(1, HS, lambda k, p=p, c=c: help_copy(p, c, k, place).wait_send())
@@ -423,6 +474,7 @@
     E, rows, H = w_gate.shape
     L, D = tokens.shape[1:]
     EL = E // R
+    HH = H // 2
     chips = R // 2
     lanes = -(-E // 128) * 128
     any_spec = pl.BlockSpec(memory_space=pl.ANY)
@@ -439,24 +491,24 @@
             vmem((L, D), BF16), vmem((L, D), BF16), vmem((D // 2, L), BF16), vmem((D // 2, L), BF16),
             vmem((L, D // 2), BF16), vmem((L, D // 2), BF16), vmem((D // 2, L), BF16), vmem((D // 2, L), BF16),
             vmem((3, E, rows, H), BF16),
-            vmem((3, S, rows, H), BF16),
-            vmem((2, D, H), BF16),
-            vmem((2, D // 2, H), BF16),
-            vmem((3, S // 2, rows, H), BF16), vmem((3, S // 2, rows, H), BF16),
-            vmem((3, R, S, rows, H), BF16),
+            vmem((6, S, rows, HH), BF16),
+            vmem((4, D, HH), BF16),
+            vmem((2, 2, D // 2, HH), BF16),
+            vmem((6, S // 2, rows, HH), BF16), vmem((6, S // 2, rows, HH), BF16),
+            vmem((6, R, S, rows, HH), BF16),
             vmem((3, EL, rows, H), BF16),
             vmem((L, D), BF16),
             vmem((R, S, lanes), F32),
             vmem((S * T, E * T), BF16),
             vmem((EL * T, R * S * T), BF16),
-            vmem((L, H), F32), vmem((L, H), F32), vmem((L, H), F32),
-            vmem((L, H), BF16), vmem((L, H), BF16),
-            vmem((3, L, H), BF16), vmem((3, L, H), BF16),
+            vmem((2, L, HH), F32), vmem((2, L, HH), F32), vmem((2, L, HH), F32),
+            vmem((2, L, HH), BF16), vmem((2, L, HH), BF16),
+            vmem((6, L, HH), BF16), vmem((6, L, HH), BF16),
             dma((4 + rows // HEAD,)), dma((4,)),
-            dma((2, S)), dma((2, S)), dma((2, S // 2)), dma((2, S // 2)),
-            dma((6,)), dma((6,)),
-            dma((3, S // 2)), dma((3, S // 2)), dma((3, Q, S // 2)), dma((3, Q, S // 2)),
-            dma((3, Q + 1, chips)), dma((3, Q + 1, chips)), dma((3, Q + 1, chips)), dma((3, Q + 1, chips)),
+            dma((4, S)), dma((4, S)), dma((2, 2, S // 2)), dma((2, 2, S // 2)),
+            dma((10,)), dma((10,)),
+            dma((6, S // 2)), dma((6, S // 2)), dma((6, Q, S // 2)), dma((6, Q, S // 2)),
+            dma((6, Q + 1, chips)), dma((6, Q + 1, chips)), dma((6, Q + 1, chips)), dma((6, Q + 1, chips)),
             dma((R,)), dma((R,)),
         ],
         compiler_params=pltpu.CompilerParams(
@@ -535,7 +587,7 @@
 
     def body(tokens, cotangent, coefficients, w_gate, w_up, w_down):
         args = (tokens, cotangent, coefficients, w_gate, w_up, w_down)
-        if w_gate.shape[1] % 128 == 0 and R % 2 == 0 and S % 2 == 0 and tokens.shape[1] % 128 == 0:
+        if w_gate.shape[1] % 128 == 0 and w_gate.shape[2] % 256 == 0 and R % 2 == 0 and S % 2 == 0 and tokens.shape[1] % 128 == 0:
             return fused(S, R, *args)
         return local(*args)
 

time: 165 us -> 166 us (level)
  the two profiles are of different devices: /device:TPU:21 before, /device:TPU:0 now
where the time goes in v6:
time: 166 us
  Pallas kernels  165 us (99%)
    pallas_call x1, Pallas kernels, fused(): pl.pallas_call(functools.partial(kernel, S, R), out_shape=(jax.ShapeDtype...  162 us

profile of v6, /device:TPU:0, one launch (start us, length us, event | category | flops | bytes accessed | tf_op | source)
XLA Modules:
  0.0 165.7 jit_solution(9911857354343683884)
XLA Ops:
  0.6 161.9 %shard_map.93 = (bf16[1,256,1024]{2,1,0:T(8,128)(2,1)}, bf16[8,128,512]{2,1,0:T(8,128)(2,1)}, bf16[8,128,512]{2,1,0:T(8,128)(2,1)}, bf16[8,128,512]{2,1,0:T(8,128)(2,1)}) custom-call(bf16[1,8,32]{2,1,0:T(8,128)(2,1)} %coef_ref.1, bf16[1,256,1024]{2,1,0:T(8,128)(2,1)} %tok_hbm.1, bf16[1,256,1024]{2,1,0:T(8,128)(2,1)} %cot_hbm.1, ...), custom_call_target="tpu_custom_call" | custom-call | flops 5368709120 | bytes 17301504 | tf_op jit(solution)/shard_map/pallas_call | solution.py:485
  162.6 3.2 %shard_map.94 = (bf16[1,256,1024]{2,1,0:T(8,128)(2,1)}, bf16[8,128,512]{2,1,0:T(8,128)(2,1)}, bf16[8,128,512]{2,1,0:T(8,128)(2,1)}, bf16[8,128,512]{2,1,0:T(8,128)(2,1)}) custom-call(bf16[1,256,1024]{2,1,0:T(8,128)(2,1)} %get-tuple-element.8.refs_0_, bf16[8,128,512]{2,1,0:T(8,128)(2,1)} %get-tuple-element.9.refs_1_, ...), custom_call_target="tpu_custom_call" | custom-call | bytes 7340032 | tf_op jit(solution)/shard_map/pallas_call | solution.py:462

commit v7 on v2

--- a/solution.py
+++ b/solution.py
@@ -190,7 +190,7 @@
     make_grads(DOWN, gt, hid_s)
     loop(1, S, lambda k: merged_copy(DOWN, k, me).wait_send())
     steps = [(p, c) for p in (DOWN, GATE, UP) for c in range(Q)]
-    AHEAD = 2
+    AHEAD = 4
     for p, c in steps[:AHEAD]:
         send(p, c)
 
@@ -215,13 +215,12 @@
     ig_copy = pltpu.make_async_copy(igv, ig_hbm.at[0], out_sem.at[3])
     outs = (gg_hbm, gu_hbm, gd_hbm)
     out_copies = [ig_copy]
-    for i in range(AHEAD, len(steps) + 4):
-        if i < len(steps):
-            sent(*steps[i - AHEAD])
-            send(*steps[i])
-        if i == AHEAD:
-            make_grads(GATE, xt, dgate_s)
-        if i == Q:
+    make_grads(GATE, xt, dgate_s)
+    for i in range(2, len(steps) + 4):
+        if i - 2 + AHEAD < len(steps):
+            sent(*steps[i - 2])
+            send(*steps[i - 2 + AHEAD])
+        if i == 3:
             make_grads(UP, xt, dup_s)
         if i == Q + 1:
             loop(0, S, input_grad)

time: 166 us -> 172 us (1.036)
  Pallas kernels: 162 us -> 168 us
    pallas_call x1, Pallas kernels: 159 us -> 165 us  [fused(): pl.pallas_call(functools.partial(kernel, S, R), out_shape=(jax.ShapeDtype...]
where the time goes in v7:
time: 172 us; the launch traced here: 169 us
  Pallas kernels  168 us (98%)
    pallas_call x1, Pallas kernels, fused(): pl.pallas_call(functools.partial(kernel, S, R), out_shape=(jax.ShapeDtype...  165 us

profile of v7, /device:TPU:21, one launch (start us, length us, event | category | flops | bytes accessed | tf_op | source)
XLA Modules:
  0.0 168.9 jit_solution(5994114787486604503)
XLA Ops:
  0.6 165.1 %shard_map.93 = (bf16[1,256,1024]{2,1,0:T(8,128)(2,1)}, bf16[8,128,512]{2,1,0:T(8,128)(2,1)}, bf16[8,128,512]{2,1,0:T(8,128)(2,1)}, bf16[8,128,512]{2,1,0:T(8,128)(2,1)}) custom-call(bf16[1,8,32]{2,1,0:T(8,128)(2,1)} %coef_ref.1, bf16[1,256,1024]{2,1,0:T(8,128)(2,1)} %tok_hbm.1, bf16[1,256,1024]{2,1,0:T(8,128)(2,1)} %cot_hbm.1, ...), custom_call_target="tpu_custom_call" | custom-call | flops 5368709120 | bytes 17301504 | tf_op jit(solution)/shard_map/pallas_call | solution.py:311
  165.7 3.2 %shard_map.94 = (bf16[1,256,1024]{2,1,0:T(8,128)(2,1)}, bf16[8,128,512]{2,1,0:T(8,128)(2,1)}, bf16[8,128,512]{2,1,0:T(8,128)(2,1)}, bf16[8,128,512]{2,1,0:T(8,128)(2,1)}) custom-call(bf16[1,256,1024]{2,1,0:T(8,128)(2,1)} %get-tuple-element.8.refs_0_, bf16[8,128,512]{2,1,0:T(8,128)(2,1)} %get-tuple-element.9.refs_1_, ...), custom_call_target="tpu_custom_call" | custom-call | bytes 7340032 | tf_op jit(solution)/shard_map/pallas_call | solution.py:288
